TPU v7x, 32 devices: a whole 2x2x4 slice. The times are simulated.
32 devices in a mesh: rep: 4 (over y, x), fsdp: 8 (over z, core).
Axes of the slice: x: 2, y: 2, z: 4, core: 2. Of those that a mesh axis runs over, the one named last changes fastest.
Arguments:
- tokens: bfloat16 [16384, 768], P(('rep', 'fsdp')), may hold values from -6 to 6
- cotangent: bfloat16 [16384, 768], P(('rep', 'fsdp')), may hold values from -6 to 6
- place: int32 [16384], P(('rep', 'fsdp')), may hold values from 0 to 4095, as said below
- seq_lengths: int32 [32, 4], P(('rep', 'fsdp')), may hold values from 0 to 512, as said below
- random_blocks: int32 [256, 12, 3], P(('rep', 'fsdp')), may hold values from 0 to 7
- owner_slot: int32 [12], replicated, may hold values from 0 to 15, as said below
- flat_weights: float32 [768, 9216], P('fsdp')
- vectors: float32 [768, 12], P('fsdp')
- moment_first: float32 [768, 12], P('fsdp')
- moment_second: float32 [768, 12], P('fsdp')
- stat_left: float32 [16, 768, 768], P('fsdp')
- stat_right: float32 [16, 768, 768], P('fsdp')
- root_left: float32 [16, 768, 768], P('fsdp')
- root_right: float32 [16, 768, 768], P('fsdp')
Outputs:
- layer_out: bfloat16 [16384, 768], P(('rep', 'fsdp'))
- input_grad: bfloat16 [16384, 768], P(('rep', 'fsdp'))
- weight_grads: float32 [768, 9216], P('fsdp')
- new_weights: float32 [768, 9216], P('fsdp')
- new_left: float32 [16, 768, 768], P('fsdp')
- new_right: float32 [16, 768, 768], P('fsdp')
- new_first: float32 [768, 12], P('fsdp')
- new_second: float32 [768, 12], P('fsdp')
- new_vectors: float32 [768, 12], P('fsdp')
Inputs may be any that keep to these rules, and one draw needn't show every extreme that they name: Within each group place is a permutation of the group's slots; slots d * 512 to (d + 1) * 512 - 1 are those of device d. Each device sends exactly 64 of its tokens to each device of its group, and those from device s take that device's slots s * 64 onward in increasing arrival order. `seq_lengths`: A pack's sequences take together at most 8 blocks; length 0 marks an unused entry; in every group some pack holds a sequence of exactly 512 tokens. `owner_slot`: Distinct; slot o lies on device o // 2 of each group.
All inputs are finite; a program needn't handle non-finite values.
Results may differ from a plain program's by a relative error of at most 0.014.
The roundings to bfloat16 on the way count: a program that leaves them out, or rounds other values in their place, can miss the bound.
Values may be sent and summed in bfloat16 or wider, within the bound.
A program may use at most 192 MiB of HBM per device.

v0:
```python
import jax
import jax.numpy as jnp
from jax import lax
from jax.sharding import PartitionSpec as P

D = 768
H = 12
HD = 64
FF = 3072
BLK = 64
NGLOB = 2
NRAND = 3
STEP = 10
SEQ_DEV = 4
TOK_DEV = 512
NBLK = 12


NORM_EPS = 1e-12
MASKED_SCORE = -1e30
STAT_DECAY = 0.5
LR_MATRIX = 0.02
LR_VECTOR = 0.1
BETA_ONE = 0.9
BETA_TWO = 0.999
ADAM_EPS = 1e-08
RMS_EPS = 1e-12
PRECISE = lax.Precision.HIGHEST


def layout(lengths):
    blocks = (lengths + (BLK - 1)) // BLK
    block_ends = jnp.cumsum(blocks)
    starts = (block_ends - blocks) * BLK
    slot_ids = jnp.arange(TOK_DEV, dtype=jnp.int32)
    seq_id = jnp.sum((slot_ids // BLK)[:, None] >= block_ends[None, :], axis=1)
    member = seq_id[:, None] == jnp.arange(SEQ_DEV, dtype=jnp.int32)[None, :]
    seq_start = jnp.sum(jnp.where(member, starts[None, :], 0), axis=1)
    length = jnp.sum(jnp.where(member, lengths[None, :], 0), axis=1)
    seq_blocks = jnp.sum(jnp.where(member, blocks[None, :], 0), axis=1)
    position = slot_ids - seq_start
    in_use = position < length
    return (seq_id, position, in_use, seq_blocks)


def random_keys(raw_picks, seq_blocks):
    per_block = seq_blocks.reshape(TOK_DEV // BLK, BLK)[:, 0]
    picked = raw_picks % jnp.maximum(per_block, 1)[:, None, None]
    return jnp.repeat(picked, BLK, axis=0)


def allowed(q_seq, q_pos, q_use, q_pick, q_slot, k_seq, k_pos, k_use, k_slot):
    q_block = q_pos // BLK
    k_block = k_pos // BLK
    same_seq = (q_seq[:, None] == k_seq[None, :]) & q_use[:, None] & k_use[None, :]
    nearby = (
        (q_block[:, None] < NGLOB)
        | (k_block[None, :] < NGLOB)
        | (jnp.abs(q_block[:, None] - k_block[None, :]) <= 1)
    )
    chosen = jnp.zeros((H, q_seq.shape[0], k_seq.shape[0]), dtype=jnp.bool_)
    for number in range(NRAND):
        chosen = chosen | (
            k_block[None, None, :] == jnp.transpose(q_pick[:, :, number])[:, :, None]
        )
    alone = jnp.logical_not(q_use)[:, None] & (q_slot[:, None] == k_slot[None, :])
    return (same_seq & nearby)[None] | same_seq[None] & chosen | alone[None]


def layer_norm(hidden, gain, shift):
    center = hidden - jnp.mean(hidden, axis=-1, keepdims=True)
    spread = jnp.mean(center * center, axis=-1, keepdims=True)
    return center * lax.rsqrt(spread + NORM_EPS) * gain + shift


def gelu_tanh(pre_act):
    return jax.nn.gelu(pre_act, approximate=True)


def contract_rows(left, right):
    return lax.dot_general(
        left, right, (((0,), (0,)), ((), ())), preferred_element_type=jnp.float32
    )


def contract_cols(left, right):
    return lax.dot_general(
        left, right, (((1,), (1,)), ((), ())), preferred_element_type=jnp.float32
    )


def body(
    tokens,
    cotangent,
    place,
    seq_lengths,
    random_blocks,
    owner_slot,
    flat_weights,
    vectors,
    moment_first,
    moment_second,
    stat_left,
    stat_right,
    root_left,
    root_right,
):
    peers = lax.axis_size("fsdp")
    share_rows = TOK_DEV // peers
    order_ids = jnp.argsort(place)
    outgoing = (
        tokens[order_ids].reshape(peers, share_rows, D),
        cotangent[order_ids].reshape(peers, share_rows, D),
    )
    arrived = (
        lax.all_to_all(outgoing[0], "fsdp", split_axis=0, concat_axis=0, tiled=True),
        lax.all_to_all(outgoing[1], "fsdp", split_axis=0, concat_axis=0, tiled=True),
    )
    inputs = arrived[0].reshape(TOK_DEV, D)
    upstream = arrived[1].reshape(TOK_DEV, D).astype(jnp.float32)
    weight_copy, vector_copy = (
        lax.all_gather(flat_weights.astype(jnp.bfloat16), "fsdp", axis=0, tiled=True),
        lax.all_gather(vectors.astype(jnp.bfloat16), "fsdp", axis=0, tiled=True),
    )
    vecs_full = vector_copy.astype(jnp.float32)
    b_up = jnp.transpose(vecs_full[:, 8:]).reshape(FF)
    seq_id, position, in_use, seq_blocks = layout(seq_lengths[0])
    picks = random_keys(random_blocks, seq_blocks)
    slot_ids = jnp.arange(TOK_DEV, dtype=jnp.int32)
    real_rows = in_use.astype(jnp.float32)[:, None]
    bias_qkv = jnp.concatenate([vecs_full[:, 0], jnp.zeros((D,), jnp.float32), vecs_full[:, 1]])
    qkv_low = (
        jnp.dot(inputs, weight_copy[:, : 3 * D], preferred_element_type=jnp.float32) + bias_qkv
    ).astype(jnp.bfloat16)
    qkv_heads = qkv_low.reshape(TOK_DEV, 3, H, HD)
    queries = qkv_heads[:, 0]
    key_heads = qkv_heads[:, 1]
    value_heads = qkv_heads[:, 2]
    block_rows = min(512, TOK_DEV)
    block_count = TOK_DEV // block_rows
    score_scale = HD ** (-0.5)

    def split_blocks(array):
        return array.reshape((block_count, block_rows) + array.shape[1:])

    block_inputs = (
        split_blocks(queries),
        split_blocks(seq_id),
        split_blocks(position),
        split_blocks(in_use),
        split_blocks(picks),
        split_blocks(slot_ids),
    )

    def scores_of(query_block, q_seq, q_pos, q_use, q_pick, q_slot):
        raw_scores = (
            jnp.einsum("qhd,khd->hqk", query_block, key_heads, preferred_element_type=jnp.float32)
            * score_scale
        )
        keep_mask = allowed(q_seq, q_pos, q_use, q_pick, q_slot, seq_id, position, in_use, slot_ids)
        return jnp.where(keep_mask, raw_scores, MASKED_SCORE)

    def forward_block(pieces):
        scores = scores_of(pieces[0], pieces[1], pieces[2], pieces[3], pieces[4], pieces[5])
        row_max = jnp.max(scores, axis=-1, keepdims=True)
        expo = jnp.exp(scores - row_max)
        row_total = jnp.sum(expo, axis=-1, keepdims=True)
        probs_low = (expo / row_total).astype(jnp.bfloat16)
        mixed_block = jnp.einsum(
            "hqk,khd->qhd", probs_low, value_heads, preferred_element_type=jnp.float32
        )
        return (mixed_block.reshape(block_rows, D), (row_max + jnp.log(row_total))[:, :, 0])

    attended, log_totals = lax.map(forward_block, block_inputs)
    mixed = attended.reshape(TOK_DEV, D).astype(jnp.bfloat16)
    branch = (
        jnp.dot(mixed, weight_copy[:, 3 * D : 4 * D], preferred_element_type=jnp.float32)
        + vecs_full[:, 2]
    )
    hidden_one = inputs.astype(jnp.float32) + branch
    x_one, norm_one_back = jax.vjp(layer_norm, hidden_one, vecs_full[:, 4], vecs_full[:, 5])
    x_one_low = x_one.astype(jnp.bfloat16)
    pre_act = (
        jnp.dot(x_one_low, weight_copy[:, 4 * D : 4 * D + FF], preferred_element_type=jnp.float32)
        + b_up
    )
    act, gelu_back = jax.vjp(gelu_tanh, pre_act)
    act_low = act.astype(jnp.bfloat16)
    ffn = contract_cols(act_low, weight_copy[:, 4 * D + FF :]) + vecs_full[:, 3]
    hidden_two = x_one + ffn
    result, norm_two_back = jax.vjp(layer_norm, hidden_two, vecs_full[:, 6], vecs_full[:, 7])
    layer_rows = (result * real_rows).astype(jnp.bfloat16)
    weight_copy = lax.all_gather(flat_weights.astype(jnp.bfloat16), "fsdp", axis=0, tiled=True)
    d_result = upstream * real_rows
    d_two, d_gain_two, d_shift_two = norm_two_back(d_result)
    d_ffn = d_two.astype(jnp.bfloat16)
    d_act = jnp.dot(d_ffn, weight_copy[:, 4 * D + FF :], preferred_element_type=jnp.float32)
    (d_pre,) = gelu_back(d_act)
    d_pre_low = d_pre.astype(jnp.bfloat16)
    grad_down = contract_rows(d_ffn, act_low)
    grad_up = contract_rows(x_one_low, d_pre_low)
    d_x_one = d_two + contract_cols(d_pre_low, weight_copy[:, 4 * D : 4 * D + FF])
    d_one, d_gain_one, d_shift_one = norm_one_back(d_x_one)
    up_sums = jnp.transpose(jnp.sum(d_pre_low.astype(jnp.float32), axis=0).reshape(FF // D, D))
    ffn_vec = jnp.concatenate(
        [
            jnp.sum(d_ffn.astype(jnp.float32), axis=0)[:, None],
            d_gain_one[:, None],
            d_shift_one[:, None],
            d_gain_two[:, None],
            d_shift_two[:, None],
            up_sums,
        ],
        axis=1,
    )
    ffn_mats = jnp.concatenate([grad_up, grad_down], axis=1)
    d_branch = d_one.astype(jnp.bfloat16)
    grad_out = contract_rows(mixed, d_branch)
    d_mixed = (
        contract_cols(d_branch, weight_copy[:, 3 * D : 4 * D])
        .astype(jnp.bfloat16)
        .reshape(TOK_DEV, H, HD)
    )

    def backward_block(carry, pieces):
        key_grad, value_grad = carry
        query_block = pieces[0]
        log_total = pieces[6]
        out_grad = pieces[7]
        scores = scores_of(pieces[0], pieces[1], pieces[2], pieces[3], pieces[4], pieces[5])
        probs = jnp.exp(scores - log_total[:, :, None])
        probs_low = probs.astype(jnp.bfloat16)
        value_grad = value_grad + jnp.einsum(
            "hqk,qhd->khd", probs_low, out_grad, preferred_element_type=jnp.float32
        )
        prob_grad = jnp.einsum(
            "qhd,khd->hqk", out_grad, value_heads, preferred_element_type=jnp.float32
        )
        score_grad = (
            probs * (prob_grad - jnp.sum(probs * prob_grad, axis=-1, keepdims=True))
        ).astype(jnp.bfloat16)
        query_grad = (
            jnp.einsum("hqk,khd->qhd", score_grad, key_heads, preferred_element_type=jnp.float32)
            * score_scale
        )
        key_grad = (
            key_grad
            + jnp.einsum(
                "hqk,qhd->khd", score_grad, query_block, preferred_element_type=jnp.float32
            )
            * score_scale
        )
        return ((key_grad, value_grad), query_grad)

    zero_heads = jnp.zeros((TOK_DEV, H, HD), jnp.float32)
    (key_grad, value_grad), query_grad = lax.scan(
        backward_block, (zero_heads, zero_heads), block_inputs + (log_totals, split_blocks(d_mixed))
    )
    d_qkv = jnp.concatenate(
        [
            query_grad.reshape(TOK_DEV, D),
            key_grad.reshape(TOK_DEV, D),
            value_grad.reshape(TOK_DEV, D),
        ],
        axis=1,
    ).astype(jnp.bfloat16)
    grad_qkv = contract_rows(inputs, d_qkv)
    d_inputs = d_one + contract_cols(d_qkv, weight_copy[:, : 3 * D])
    qkv_sums = jnp.sum(d_qkv.astype(jnp.float32), axis=0)
    attn_vec = jnp.stack(
        [qkv_sums[:D], qkv_sums[2 * D :], jnp.sum(d_branch.astype(jnp.float32), axis=0)], axis=1
    )
    attn_mats = jnp.concatenate([grad_qkv, grad_out], axis=1)
    mat_shard, vec_shard = (
        lax.psum_scatter(
            jnp.concatenate([attn_mats, ffn_mats], axis=1), "fsdp", scatter_dimension=0, tiled=True
        ),
        lax.psum_scatter(
            jnp.concatenate([attn_vec, ffn_vec], axis=1), "fsdp", scatter_dimension=0, tiled=True
        ),
    )
    mat_part = lax.psum_scatter(
        mat_shard.astype(jnp.bfloat16), "rep", scatter_dimension=1, tiled=True
    ).astype(jnp.float32)
    vec_shard = lax.psum(vec_shard, "rep")
    mat_shard = lax.all_gather(mat_part.astype(jnp.bfloat16), "rep", axis=1, tiled=True).astype(
        mat_part.dtype
    )
    grad_rows = d_inputs.astype(jnp.bfloat16)
    back_pair = (
        lax.all_to_all(
            layer_rows.reshape(peers, share_rows, D),
            "fsdp",
            split_axis=0,
            concat_axis=0,
            tiled=True,
        ),
        lax.all_to_all(
            grad_rows.reshape(peers, share_rows, D), "fsdp", split_axis=0, concat_axis=0, tiled=True
        ),
    )
    layer_out = (
        jnp.zeros((TOK_DEV, D), jnp.bfloat16).at[order_ids].set(back_pair[0].reshape(TOK_DEV, D))
    )
    input_grad = (
        jnp.zeros((TOK_DEV, D), jnp.bfloat16).at[order_ids].set(back_pair[1].reshape(TOK_DEV, D))
    )
    slot_count = stat_left.shape[0]
    rows_dev = flat_weights.shape[0]
    targets = (
        jnp.arange(slot_count, dtype=jnp.int32)[:, None, None]
        + slot_count * jnp.arange(peers, dtype=jnp.int32)[None, :, None]
    )
    select = (owner_slot[None, None, :] == targets).astype(jnp.float32)
    grad_pieces = mat_shard.reshape(rows_dev, NBLK, D)
    outbound = jnp.einsum("snb,rbc->snrc", select, grad_pieces, precision=PRECISE)
    inbound = lax.all_to_all(
        outbound.astype(jnp.bfloat16), "fsdp", split_axis=1, concat_axis=1, tiled=True
    ).astype(outbound.dtype)
    grad_blocks = inbound.reshape(slot_count, D, D)
    new_left = STAT_DECAY * stat_left + (1.0 - STAT_DECAY) * jnp.einsum(
        "sij,skj->sik", grad_blocks, grad_blocks, precision=PRECISE
    )
    new_right = STAT_DECAY * stat_right + (1.0 - STAT_DECAY) * jnp.einsum(
        "sji,sjk->sik", grad_blocks, grad_blocks, precision=PRECISE
    )
    left_applied = jnp.einsum("sij,sjk->sik", root_left, grad_blocks, precision=PRECISE)
    direction = jnp.einsum("sij,sjk->sik", left_applied, root_right, precision=PRECISE)
    update = direction * lax.rsqrt(
        jnp.mean(direction * direction, axis=(1, 2), keepdims=True) + RMS_EPS
    )
    returned = lax.all_to_all(
        update.reshape(slot_count, peers, rows_dev, D).astype(jnp.bfloat16),
        "fsdp",
        split_axis=1,
        concat_axis=1,
        tiled=True,
    ).astype(jnp.float32)
    step_matrix = jnp.einsum("snb,snrc->rbc", select, returned, precision=PRECISE).reshape(
        rows_dev, NBLK * D
    )
    new_weights = flat_weights - LR_MATRIX * step_matrix
    first_bias = 1.0 - BETA_ONE**STEP
    second_bias = 1.0 - BETA_TWO**STEP
    new_first = BETA_ONE * moment_first + (1.0 - BETA_ONE) * vec_shard
    new_second = BETA_TWO * moment_second + (1.0 - BETA_TWO) * vec_shard * vec_shard
    first_fixed = new_first / first_bias
    second_fixed = new_second / second_bias
    new_vectors = vectors - LR_VECTOR * first_fixed / (jnp.sqrt(second_fixed) + ADAM_EPS)
    return (
        layer_out,
        input_grad,
        mat_shard,
        new_weights,
        new_left,
        new_right,
        new_first,
        new_second,
        new_vectors,
    )


def solution(mesh):
    in_specs = (
        P(("rep", "fsdp"), None),
        P(("rep", "fsdp"), None),
        P(("rep", "fsdp")),
        P(("rep", "fsdp"), None),
        P(("rep", "fsdp"), None, None),
        P(),
        P("fsdp", None),
        P("fsdp", None),
        P("fsdp", None),
        P("fsdp", None),
        P("fsdp", None, None),
        P("fsdp", None, None),
        P("fsdp", None, None),
        P("fsdp", None, None),
    )
    out_specs = (
        P(("rep", "fsdp"), None),
        P(("rep", "fsdp"), None),
        P("fsdp", None),
        P("fsdp", None),
        P("fsdp", None, None),
        P("fsdp", None, None),
        P("fsdp", None),
        P("fsdp", None),
        P("fsdp", None),
    )
    return jax.shard_map(body, mesh=mesh, in_specs=in_specs, out_specs=out_specs, check_vma=False)
```

profile of v0, /device:TPU:9, one launch (start us, length us, event | category | flops | bytes accessed | tf_op | source)
XLA Modules:
  0.0 867.8 jit_solution(5962547240004465786)
XLA Ops:
  7.2 3.5 convert_element_type.117
  10.8 3.8 sort.17
  15.2 2.7 gather_fusion
  17.9 5.6 all-to-all-start
  23.5 2.7 gather_fusion.1
  26.2 47.1 %all-gather = bf16[8,96,12]{1,2,0:T(8,128)(2,1)S(1)} all-gather(bf16[1,96,12]{1,2,0:T(8,128)(2,1)S(1)} %convert_bitcast_fusion), channel_id=1, replica_groups=mesh['rep'=4,'fsdp'=8] {'fsdp'}, dimensions={0}, use_global_device_ids=true | all-gather | bytes 20736 | tf_op jit(solution)/shard_map/all_gather | solution.py:123
  76.5 6.8 all-to-all-start.2
  83.3 86.7 %all-gather.4.cloned.1.call-done = bf16[768,9216]{1,0:T(8,128)(2,1)} async-done(((bf16[96,9216]{1,0:T(8,128)(2,1)}), bf16[768,9216]{1,0:T(8,128)(2,1)}) %all-gather.4.cloned.1.call-update) | async-done | bytes 14155792 | tf_op jit(solution)/shard_map/all_gather | solution.py:122
  170.0 5.4 fusion.13
  175.4 3.0 copy.95
  178.4 7.5 fusion.80
  187.8 2.7 copy-done.2
  192.9 2.5 fusion.81
  195.8 5.2 fusion.20
  201.0 8.9 %fusion.82 = (f32[512]{0:T(512)S(1)}, f32[512,768]{1,0:T(8,128)S(1)}) fusion(f32[768]{0:T(1024)S(1)} %get-tuple-element.99, bf16[768,9216]{1,0:T(8,128)(2,1)} %all-gather.4.cloned.1.call-done, f32[512,3072]{1,0:T(8,128)S(1)} %fusion.20, f32[3072]{0:T(1024)S(1)} %add.250, f32[768]{0:T(1024)S(1)} %get-tuple-element.100, f32[768]{0:T(1024)S(1)} %get-tuple-element.101, ...), kind=kOutput, calls=%fused_computation.182 | convolution fusion | flops 2434399744 | bytes 14183424 | tf_op jit(solution)/shard_map/dot_general | solution.py:87
  214.3 8.4 convert_reduce_fusion
  222.8 6.7 multiply_reduce_fusion.4
  231.5 3.0 convolution_convert_fusion.1
  235.9 7.7 fusion.38
  243.6 8.9 %multiply_reduce_fusion = (f32[12,512]{1,0:T(8,128)S(1)}, f32[12,512,512]{1,2,0:T(8,128)}) fusion(f32[12,512,512]{1,2,0:T(8,128)} %copy-done.2, f32[12,512]{1,0:T(8,128)S(1)} %log_add_fusion, bf16[512,12,64]{0,2,1:T(8,128)(2,1)S(1)} %bitcast.145, bf16[512,3,12,64]{0,3,2,1:T(8,128)(2,1)S(1)} %bitcast.140), kind=kOutput, calls=%fused_computation.6 | convolution fusion | flops 412084224 | bytes 26796032 | tf_op jit(solution)/shard_map/while/body/eval_jaxpr/qhd,khd->hqk/dot_general | solution.py:236
  252.5 6.8 multiply_convert_fusion
  263.5 5.4 fusion.73
  268.9 5.8 fusion.70
  276.0 4.9 fusion.69
  280.9 19.5 %pad_maximum_fusion = f32[768,9216]{1,0:T(8,128)} fusion(f32[768,3072]{1,0:T(8,128)} %fusion.73, f32[768,3072]{1,0:T(8,128)} %fusion.70, f32[768,768]{1,0:T(8,128)S(1)} %fusion.83, f32[768,2304]{1,0:T(8,128)} %fusion.69), kind=kLoop, calls=%fused_computation.4 | loop fusion | flops 21233664 | bytes 56623104 | tf_op jit(solution)/shard_map/concatenate | solution.py:276
  300.5 279.0 %reduce-scatter.6.cloned.1.call-done = f32[96,9216]{1,0:T(8,128)} async-done(((f32[768,9216]{1,0:T(8,128)}), f32[96,9216]{1,0:T(8,128)}) %reduce-scatter.6.cloned.1.call-update) | async-done | bytes 3538960 | tf_op jit(solution)/shard_map/reduce_scatter | solution.py:275
  579.4 3.4 convert_element_type.139
  582.9 32.5 %reduce-scatter.8.cloned.1.call-done = bf16[96,2304]{1,0:T(8,128)(2,1)} async-done(((bf16[96,9216]{1,0:T(8,128)(2,1)}), bf16[96,2304]{1,0:T(8,128)(2,1)}) %reduce-scatter.8.cloned.1.call-update) | async-done | bytes 442384 | tf_op jit(solution)/shard_map/reduce_scatter | solution.py:282
  615.5 34.3 %all-gather.6.cloned.1.call-done = bf16[96,9216]{1,0:T(8,128)(2,1)} async-done(((bf16[96,2304]{1,0:T(8,128)(2,1)}), bf16[96,9216]{1,0:T(8,128)(2,1)}) %all-gather.6.cloned.1.call-update) | async-done | bytes 1769488 | tf_op jit(solution)/shard_map/all_gather | solution.py:286
  649.7 3.0 reshape.669
  654.1 57.0 %all_to_all.30 = bf16[2,8,96,768]{3,2,0,1:T(8,128)(2,1)} all-to-all(bf16[2,8,96,768]{3,2,0,1:T(8,128)(2,1)S(1)} %copy.103), channel_id=1, replica_groups=mesh['rep'=4,'fsdp'=8] {'fsdp'}, dimensions={1} | all-to-all | bytes 4718592 | tf_op jit(solution)/shard_map/all_to_all | solution.py:317
  711.1 7.2 all-to-all-start.1
  718.4 5.6 add_convert_fusion
  724.1 11.7 %all-to-all-done.1 = bf16[8,64,768]{2,1,0:T(8,128)(2,1)} async-done(((bf16[8,64,768]{2,1,0:T(8,128)(2,1)}), bf16[8,64,768]{2,1,0:T(8,128)(2,1)}, u32[]{:S(2)}, u32[]{:S(2)}) %all-to-all-start.1) | async-done | bytes 786464 | tf_op jit(solution)/shard_map/all_to_all | solution.py:291
  735.8 8.0 all-to-all-start.3
  743.8 7.7 fusion.84
  751.5 13.5 %multiply_reduce_fusion.1 = (f32[2]{0:T(128)S(1)}, f32[2,768,768]{2,1,0:T(8,128)S(1)}) fusion(f32[2,768,768]{1,2,0:T(8,128)S(1)} %fusion.84, f32[2,768,768]{2,1,0:T(8,128)} %param.27), kind=kOutput, calls=%fused_computation.33 | convolution fusion | flops 10873995264 | bytes 14155784 | tf_op jit(solution)/shard_map/sij,sjk->sik/dot_general | solution.py:328
  765.5 3.8 copy.107
  769.4 5.3 all-to-all-start.5
  778.5 28.3 %reduce-scatter.10.cloned.1.call-done = f32[96,12]{1,0:T(8,128)} async-done(((f32[768,12]{1,0:T(8,128)}), f32[96,12]{1,0:T(8,128)}) %reduce-scatter.10.cloned.1.call-update) | async-done | bytes 4624
  807.7 21.2 %psum.7 = f32[96,12]{0,1:T(8,128)S(1)} all-reduce(f32[96,12]{0,1:T(8,128)S(1)} %copy.121), channel_id=1, replica_groups=mesh['rep'=4,'fsdp'=8] {'rep'}, use_global_device_ids=true, to_apply=%region_31.32 | all-reduce | flops 1152 | bytes 9216 | tf_op jit(solution)/shard_map/psum | solution.py:285
  829.6 4.1 scatter_custom_fusion
  833.7 4.1 scatter_custom_fusion.1
  837.8 3.7 convert_element_type.140
  841.6 6.6 add_multiply_fusion.1
  848.2 4.4 add_multiply_fusion
  852.6 3.5 bitcast_multiply_fusion
  856.1 2.5 copy.122
  (192 shorter events, 31.2 us)
Async XLA Ops:
  7.2 8.0 copy-start
  7.2 3.6 copy-start.36
  7.2 162.8 %all-gather.4.cloned.1.call-start = ((), (), s32[]{:S(2)}) async-start(), calls=%async_computation.9 | async-start | bytes 15925248 | tf_op jit(solution)/shard_map/all_gather | solution.py:122
  15.1 8.4 copy-start.3
  17.9 58.7 %all-to-all-start = ((bf16[8,64,768]{2,1,0:T(8,128)(2,1)}), bf16[8,64,768]{2,1,0:T(8,128)(2,1)S(1)}, u32[]{:S(2)}, u32[]{:S(2)}) async-start(bf16[8,64,768]{2,1,0:T(8,128)(2,1)} %bitcast), calls=%async_computation | async-start | bytes 1572864 | tf_op jit(solution)/shard_map/all_to_all | solution.py:116
  23.5 2.7 copy-start.25
  23.5 50.0 %copy-start.37 = (s32[1,4]{1,0:T(1,128)S(1)}, s32[1,4]{1,0:T(1,128)}, u32[]{:S(2)}) copy-start(s32[1,4]{1,0:T(1,128)} %param.17) | copy-start | bytes 52
  23.5 50.6 %copy-start.31 = (s32[8,12,3]{1,0,2:T(8,128)S(1)}, s32[8,12,3]{1,0,2:T(8,128)}, u32[]{:S(2)}) copy-start(s32[8,12,3]{1,0,2:T(8,128)} %param.18) | copy-start | bytes 3460
  76.5 93.5 %copy-start.18 = (bf16[8,64,768]{2,1,0:T(8,128)(2,1)}, bf16[8,64,768]{2,1,0:T(8,128)(2,1)S(1)}, u32[]{:S(2)}) copy-start(bf16[8,64,768]{2,1,0:T(8,128)(2,1)S(1)} %all-to-all-done) | copy-start | bytes 2359300
  76.5 133.7 %all-to-all-start.2 = ((bf16[8,64,768]{2,1,0:T(8,128)(2,1)}), bf16[8,64,768]{2,1,0:T(8,128)(2,1)S(1)}, u32[]{:S(2)}, u32[]{:S(2)}) async-start(bf16[8,64,768]{2,1,0:T(8,128)(2,1)} %bitcast.24), calls=%async_computation.2 | async-start | bytes 1572864 | tf_op jit(solution)/shard_map/all_to_all | solution.py:117
  83.3 496.2 %reduce-scatter.6.cloned.1.call-start = ((), (), s32[]{:S(2)}) async-start(), calls=%async_computation.10 | async-start | bytes 31850496 | tf_op jit(solution)/shard_map/reduce_scatter | solution.py:275
  178.4 9.4 %copy-start.5 = (bf16[512,2304]{0,1:T(8,128)(2,1)}, bf16[512,2304]{0,1:T(8,128)(2,1)S(1)}, u32[]{:S(2)}) copy-start(bf16[512,2304]{0,1:T(8,128)(2,1)S(1)} %copy.95) | copy-start | bytes 7077892
  185.9 4.6 copy-start.2
  192.9 8.0 copy-start.23
  195.4 5.5 copy-start.10
  201.0 8.9 %copy-start.40 = (f32[512,3072]{1,0:T(8,128)}, f32[512,3072]{1,0:T(8,128)S(1)}, u32[]{:S(2)}) copy-start(f32[512,3072]{1,0:T(8,128)S(1)} %fusion.20) | copy-start | bytes 18874372
  210.9 3.4 copy-start.41
  212.8 9.9 %copy-start.21 = (bf16[512,768]{1,0:T(8,128)(2,1)}, bf16[512,768]{1,0:T(8,128)(2,1)S(1)}, u32[]{:S(2)}) copy-start(bf16[512,768]{1,0:T(8,128)(2,1)S(1)} %get-tuple-element.112) | copy-start | bytes 2359300
  214.3 8.5 copy-start.11
  222.7 6.7 copy-start.38
  235.9 7.7 copy-start.6
  235.9 16.6 %slice-start = ((s8[12582912]{0:T(1024)(128)(4,1)}), s8[4194304]{0:T(1024)(128)(4,1)S(1)}, s32[]{:S(2)}) async-start(s8[12582912]{0:T(1024)(128)(4,1)} %bitcast.131), calls=%async_computation.14 | async-start | bytes 8388608
  235.9 16.6 %slice-start.1 = ((s8[12582912]{0:T(1024)(128)(4,1)}), s8[4194304]{0:T(1024)(128)(4,1)S(1)}, s32[]{:S(2)}) async-start(s8[12582912]{0:T(1024)(128)(4,1)} %bitcast.131), calls=%async_computation.15 | async-start | bytes 8388608
  243.6 8.9 %slice-start.2 = ((s8[12582912]{0:T(1024)(128)(4,1)}), s8[4194304]{0:T(1024)(128)(4,1)S(1)}, s32[]{:S(2)}) async-start(s8[12582912]{0:T(1024)(128)(4,1)} %bitcast.131), calls=%async_computation.16 | async-start | bytes 8388608
  259.3 3.2 slice-start.5
  261.3 14.1 %copy-start.17 = (bf16[12,64,512]{2,1,0:T(8,128)(2,1)}, bf16[12,64,512]{2,1,0:T(8,128)(2,1)S(1)}, u32[]{:S(2)}) copy-start(bf16[12,64,512]{2,1,0:T(8,128)(2,1)S(1)} %multiply_convert_fusion.3) | copy-start | bytes 2359300
  263.5 11.9 %copy-start.8 = (bf16[12,64,512]{2,1,0:T(8,128)(2,1)}, bf16[12,64,512]{2,1,0:T(8,128)(2,1)S(1)}, u32[]{:S(2)}) copy-start(bf16[12,64,512]{2,1,0:T(8,128)(2,1)S(1)} %multiply_convert_fusion.4) | copy-start | bytes 2359300
  263.5 5.4 copy-start.39
  268.9 5.8 copy-start.16
  268.9 5.8 copy-start.24
  300.4 315.0 %reduce-scatter.8.cloned.1.call-start = ((), (), s32[]{:S(2)}) async-start(), calls=%async_computation.11 | async-start | bytes 2211840 | tf_op jit(solution)/shard_map/reduce_scatter | solution.py:282
  582.8 69.9 %copy-start.35 = (s32[12]{0:T(128)S(1)}, s32[12]{0:T(128)}, u32[]{:S(2)}) copy-start(s32[12]{0:T(128)} %param.19) | copy-start | bytes 148
  582.9 66.9 %all-gather.6.cloned.1.call-start = ((), (), s32[]{:S(2)}) async-start(), calls=%async_computation.12 | async-start | bytes 2211840 | tf_op jit(solution)/shard_map/all_gather | solution.py:286
  654.1 64.3 %copy-start.9 = (bf16[12,64,512]{2,1,0:T(8,128)(2,1)S(1)}, bf16[12,64,512]{2,1,0:T(8,128)(2,1)}, u32[]{:S(2)}) copy-start(bf16[12,64,512]{2,1,0:T(8,128)(2,1)} %copy-done.8) | copy-start | bytes 2359300
  654.1 64.3 %copy-start.13 = (f32[512,768]{1,0:T(8,128)S(1)}, f32[512,768]{1,0:T(8,128)}, u32[]{:S(2)}) copy-start(f32[512,768]{1,0:T(8,128)} %copy-done.12) | copy-start | bytes 4718596
  711.1 24.6 %all-to-all-start.1 = ((bf16[8,64,768]{2,1,0:T(8,128)(2,1)}), bf16[8,64,768]{2,1,0:T(8,128)(2,1)}, u32[]{:S(2)}, u32[]{:S(2)}) async-start(bf16[8,64,768]{2,1,0:T(8,128)(2,1)} %bitcast.154), calls=%async_computation.1 | async-start | bytes 1572864 | tf_op jit(solution)/shard_map/all_to_all | solution.py:291
  718.4 5.6 copy-start.7
  735.8 33.6 %all-to-all-start.3 = ((bf16[8,64,768]{2,1,0:T(8,128)(2,1)}), bf16[8,64,768]{2,1,0:T(8,128)(2,1)}, u32[]{:S(2)}, u32[]{:S(2)}) async-start(bf16[8,64,768]{2,1,0:T(8,128)(2,1)} %bitcast.161), calls=%async_computation.3 | async-start | bytes 1572864 | tf_op jit(solution)/shard_map/all_to_all | solution.py:298
  765.5 9.4 %copy-start.30 = (s32[512]{0:T(512)S(1)}, s32[512]{0:T(512)}, u32[]{:S(2)}) copy-start(s32[512]{0:T(512)} %copy-done.29) | copy-start | bytes 6148
  769.4 5.6 copy-start.28
  769.4 59.6 %copy-start.26 = (f32[96,12]{0,1:T(8,128)S(1)}, f32[96,12]{0,1:T(8,128)}, u32[]{:S(2)}) copy-start(f32[96,12]{0,1:T(8,128)} %param.21) | copy-start | bytes 13828
  769.4 59.6 %copy-start.32 = (f32[96,12]{0,1:T(8,128)S(1)}, f32[96,12]{0,1:T(8,128)}, u32[]{:S(2)}) copy-start(f32[96,12]{0,1:T(8,128)} %param.23) | copy-start | bytes 13828
  769.4 59.6 %copy-start.33 = (f32[96,12]{0,1:T(8,128)S(1)}, f32[96,12]{0,1:T(8,128)}, u32[]{:S(2)}) copy-start(f32[96,12]{0,1:T(8,128)} %param.22) | copy-start | bytes 13828
  769.4 83.2 %all-to-all-start.5 = ((bf16[2,8,96,768]{3,0,2,1:T(2,128)(2,1)}), bf16[2,8,96,768]{3,0,2,1:T(2,128)(2,1)}, u32[]{:S(2)}, u32[]{:S(2)}) async-start(bf16[2,8,96,768]{3,0,2,1:T(2,128)(2,1)} %copy.107), calls=%async_computation.7 | async-start | bytes 4718592 | tf_op jit(solution)/shard_map/all_to_all | solution.py:332
  774.6 32.2 %reduce-scatter.10.cloned.1.call-start = ((), (), s32[]{:S(2)}) async-start(), calls=%async_computation.13 | async-start | bytes 442368
  837.8 10.3 %slice-start.3 = ((s8[4718592]{0:T(1024)(128)(4,1)}), s8[4194304]{0:T(1024)(128)(4,1)S(1)}, s32[]{:S(2)}) async-start(s8[4718592]{0:T(1024)(128)(4,1)} %bitcast.149), calls=%async_computation.17 | async-start | bytes 8388608
  841.6 6.6 slice-start.4
  856.1 2.5 copy-start.4
  (11 other events, 14.9 us)
Sparse Core Ops, SparseCore 0:
  10.9 159.0 all-gather.3
  300.5 278.8 reduce-scatter.5
  583.0 32.3 reduce-scatter.7
  617.1 32.5 all-gather.5
  778.6 28.1 reduce-scatter.9
where the time goes:
time: 874 us; the launch traced here: 868 us
  waiting for transfers between devices  473 us (54%)
  matrix products  129 us (15%)
  blocking collectives  125 us (14%)
  other arithmetic  54.6 us (6%)
  local copies, waits for them, and re-layouts  38.3 us (4%)
  starting transfers between devices  33.3 us (4%)
  between operations  15.1 us (2%)
    reduce_scatter x1, waiting for transfers between devices, body(): lax.psum_scatter(jnp.concatenate([attn_mats, ffn_mats], axis=1), 'fsdp',...  279 us
    all_gather x1, waiting for transfers between devices, body(): lax.all_gather(flat_weights.astype(jnp.bfloat16), 'fsdp', axis=0, tiled=T...  86.7 us
    all_to_all x1, blocking collectives, body(): lax.all_to_all(outbound.astype(jnp.bfloat16), 'fsdp', split_axis=1, conca...  57 us
    all_gather x1, blocking collectives, body(): lax.all_gather(vectors.astype(jnp.bfloat16), 'fsdp', axis=0, tiled=True)  47.1 us
    all_gather x1, waiting for transfers between devices, body(): lax.all_gather(mat_part.astype(jnp.bfloat16), 'rep', axis=1, tiled=True)  34.3 us
    reduce_scatter x1, waiting for transfers between devices, body(): lax.psum_scatter(mat_shard.astype(jnp.bfloat16), 'rep', scatter_dimension...  32.5 us
    unnamed x6, waiting for transfers between devices  28.4 us
    dot_general x4, matrix products, contract_cols(): lax.dot_general(left, right, (((1,), (1,)), ((), ())), preferred_element_...  24.1 us
  transfers between devices with their start and end apart: 10, of which 6 were waited for; matrix products, arithmetic and copies ran while one was open for 13% of the time, Pallas kernels for 0%

commit v1 on v0

--- a/solution.py
+++ b/solution.py
@@ -1,6 +1,10 @@
+import functools
+
 import jax
 import jax.numpy as jnp
 from jax import lax
+from jax.experimental import pallas as pl
+from jax.experimental.pallas import tpu as pltpu
 from jax.sharding import PartitionSpec as P
 
 D = 768
@@ -89,7 +93,831 @@
     )
 
 
-def body(
+MESH = pl.DeviceIdType.MESH
+HALF = 48
+GCOLS = 3072
+JCOLS = 384
+MIB = 2**20
+
+
+class Here:
+    def __init__(self):
+        r, f = lax.axis_index("rep"), lax.axis_index("fsdp")
+        self.r, self.f = r, f
+        self.x, self.y = lax.rem(r, 2), lax.div(r, 2)
+        self.z, self.c = lax.div(f, 2), lax.rem(f, 2)
+        self.to_x = (r + 1 - 2 * self.x, f)
+        self.to_y = (r + 2 - 4 * self.y, f)
+        self.to_core = (r, f + 1 - 2 * self.c)
+
+    def z_plus(self, step):
+        return lax.rem(self.z + step, 4)
+
+    def along(self, step):
+        return (self.r, 2 * self.z_plus(step) + self.c)
+
+    def peer(self, step):
+        return lax.rem(self.f + step, 8)
+
+    def greet(self):
+        barrier = pltpu.get_barrier_semaphore()
+        friends = [self.to_x, self.to_y] + [(self.r, self.peer(s)) for s in range(1, 8)]
+        for friend in friends:
+            pl.semaphore_signal(barrier, inc=1, device_id=friend, device_id_type=MESH)
+        return lambda: pl.semaphore_wait(barrier, len(friends))
+
+
+def send(src, dst, send_sem, recv_sem, device):
+    copy = pltpu.make_async_remote_copy(
+        src_ref=src,
+        dst_ref=dst,
+        send_sem=send_sem,
+        recv_sem=recv_sem,
+        device_id=device,
+        device_id_type=MESH,
+    )
+    copy.start()
+    return copy
+
+
+def local(src, dst, sem):
+    copy = pltpu.make_async_copy(src, dst, sem)
+    copy.start()
+    return copy
+
+
+def cols(start, width):
+    return pl.ds(pl.multiple_of(start, 128), width)
+
+
+def gather_kernel(
+    tok, cot, wf, vec,
+    w0, w1, w2, tok_in, cot_in, vec_in,
+    wl, zs, zr, xs, xr, ys, yr, ds, dr, cs, cr, ls, ts, tr,
+):
+    here = Here()
+    wait_all = here.greet()
+    for g in range(3):
+        for h in range(2):
+            span = slice(g * GCOLS, (g + 1) * GCOLS)
+            wl[h, :, span] = wf[h, :, span].astype(jnp.bfloat16)
+    x, y, z, c, f = here.x, here.y, here.z, here.c, here.f
+    whole = [w0, w1, w2]
+    stays = [
+        local(wl.at[:, :, g * GCOLS : (g + 1) * GCOLS], whole[g].at[z, c], ls.at[g]) for g in range(3)
+    ]
+    stays.append(local(tok.at[f], tok_in.at[f], ls.at[3]))
+    stays.append(local(cot.at[f], cot_in.at[f], ls.at[4]))
+    stays.append(local(vec, vec_in.at[f], ls.at[5]))
+    wait_all()
+    wide = GCOLS // 2
+    sent = []
+
+    def z_send(g):
+        out = []
+        for step in (1, 2, 3):
+            out.append(
+                send(
+                    wl.at[x, :, cols(g * GCOLS + y * wide, wide)],
+                    whole[g].at[z, c, x, :, cols(y * wide, wide)],
+                    zs.at[g, step - 1],
+                    zr.at[g, step - 1],
+                    here.along(step),
+                )
+            )
+        sent.extend(out)
+        return out
+
+    def rows_out(table, landing, number):
+        out = []
+        for step in range(1, 8):
+            to = here.peer(step)
+            src = table if number == 2 else table.at[to]
+            out.append(
+                send(src, landing.at[f], ts.at[number, step - 1], tr.at[number, step - 1], (here.r, to))
+            )
+        sent.extend(out)
+        return out
+
+    def plane(g, copies):
+        out = []
+        for step in (1, 2, 3):
+            copies[step - 1].wait_recv()
+            src = lax.rem(z + 4 - step, 4)
+            part = whole[g].at[src, c, x, :, cols(y * wide, wide)]
+            xc = send(part, part, xs.at[g, step - 1], xr.at[g, step - 1], here.to_x)
+            yc = send(part, part, ys.at[g, step - 1], yr.at[g, step - 1], here.to_y)
+            out.append((xc, yc))
+            sent.extend([xc, yc])
+        return out
+
+    def core(g, number, h, j):
+        part = whole[g].at[:, c, h, :, cols(j * wide, wide)]
+        copy = send(part, part, cs.at[g, number], cr.at[g, number], here.to_core)
+        sent.append(copy)
+        return copy
+
+    def diagonal(g, copies):
+        out = []
+        core_copies = [core(g, 0, x, y)]
+        for step in (1, 2, 3):
+            src = lax.rem(z + 4 - step, 4)
+            xc, yc = copies[step - 1]
+            xc.wait_recv()
+            part = whole[g].at[src, c, 1 - x, :, cols(y * wide, wide // 2)]
+            out.append(send(part, part, ds.at[g, 0, step - 1], dr.at[g, 0, step - 1], here.to_y))
+            yc.wait_recv()
+            part = whole[g].at[src, c, x, :, cols((1 - y) * wide + wide // 2, wide // 2)]
+            out.append(send(part, part, ds.at[g, 1, step - 1], dr.at[g, 1, step - 1], here.to_x))
+        sent.extend(out)
+        core_copies.append(core(g, 1, 1 - x, y))
+        core_copies.append(core(g, 2, x, 1 - y))
+        for copy in out:
+            copy.wait_recv()
+        core_copies.append(core(g, 3, 1 - x, 1 - y))
+        return core_copies
+
+    z0 = z_send(0)
+    small = rows_out(vec, vec_in, 2)
+    z1 = z_send(1)
+    for g in range(3):
+        stays[g].wait()
+    p0 = plane(0, z0)
+    t0 = rows_out(tok, tok_in, 0)
+    p1 = plane(1, z1)
+    z2 = z_send(2)
+    last = diagonal(0, p0)
+    t1 = rows_out(cot, cot_in, 1)
+    last += diagonal(1, p1)
+    p2 = plane(2, z2)
+    last += diagonal(2, p2)
+    for copy in last + small + t0 + t1:
+        copy.wait_recv()
+    for copy in sent:
+        copy.wait_send()
+    for copy in stays[3:]:
+        copy.wait()
+
+
+def gather_all(tok, cot, flat_weights, vec):
+    any_spec = pl.BlockSpec(memory_space=pl.ANY)
+    vmem = pl.BlockSpec(memory_space=pltpu.VMEM)
+    dma = pltpu.SemaphoreType.DMA
+    shape = jax.ShapeDtypeStruct
+    low = jnp.bfloat16
+    return pl.pallas_call(
+        gather_kernel,
+        out_shape=[shape((4, 2, 2, HALF, GCOLS), low)] * 3
+        + [shape((8, 64, D), low)] * 2
+        + [shape((8, 96, 128), low)],
+        in_specs=[any_spec, any_spec, vmem, any_spec],
+        out_specs=[any_spec] * 6,
+        scratch_shapes=[
+            pltpu.VMEM((2, HALF, 3 * GCOLS), low),
+            dma((3, 3)), dma((3, 3)), dma((3, 3)), dma((3, 3)), dma((3, 3)), dma((3, 3)),
+            dma((3, 2, 3)), dma((3, 2, 3)), dma((3, 4)), dma((3, 4)),
+            dma((6,)), dma((3, 7)), dma((3, 7)),
+        ],
+        compiler_params=pltpu.CompilerParams(
+            collective_id=0, has_side_effects=True, vmem_limit_bytes=32 * MIB
+        ),
+        name="gather_all",
+    )(tok, cot, flat_weights.reshape(2, HALF, 3 * GCOLS), vec)
+
+
+def update_kernel(
+    block_of, owner,
+    gq, go, gu, gd, vec, rows_a, rows_b, outrow, root_l, root_r, stat_l, stat_r, wf, vecs, mom1, mom2,
+    layer_out, input_grad, wg, nw, new_l, new_r, out1, out2, outv,
+    G, Rc, A1, A2, B1, B2, ZR, F, FX, FY, FD, SO, Gs, Lb, Rb, stg, Pf, UL, UN,
+    ta, tb, vb, vr, vt,
+    gl, cs, cr, a1s, a1r, b1s, b1r, a2s, a2r, b2s, b2r, zs, zr,
+    fs, fr, ts, tr, ss, sr, ps, pr, us, ur, qs, qr, vs, vrs, ls, ks,
+):
+    low, f32 = jnp.bfloat16, jnp.float32
+    here = Here()
+    wait_all = here.greet()
+    x, y, z, c, f, r = here.x, here.y, here.z, here.c, here.f, here.r
+    W = GCOLS // 2
+    loads = []
+    sources = [(gq, 0)] * 3 + [(go, 3)] + [(gu, 4)] * 4 + [(gd, 8)] * 4
+    order = [8, 9, 10, 11, 4, 5, 6, 7, 0, 1, 2, 3]
+    by_block = {}
+    for b in order:
+        ref, first = sources[b]
+        by_block[b] = [
+            local(
+                ref.at[:, :, :, :, pl.ds((b - first) * D + j * JCOLS, JCOLS)],
+                G.at[j, :, :, :, :, pl.ds(b * JCOLS, JCOLS)],
+                gl.at[b, j],
+            )
+            for j in range(2)
+        ]
+    stage = [local(root_l.at[t], stg.at[t], ks.at[t]) for t in range(2)]
+    vb[0] = vec[...]
+    wait_all()
+    sent = []
+    got = []
+    vec_copy = send(vb.at[0], vr.at[0], vs.at[0], vrs.at[0], here.to_core)
+    sent.append(vec_copy)
+
+    def span(g):
+        return pl.ds(g * W, W)
+
+    def c_send(g):
+        for b in range(4 * g, 4 * g + 4):
+            for copy in by_block[b]:
+                copy.wait()
+        copy = send(
+            G.at[:, :, 1 - c, :, :, span(g)], Rc.at[:, :, :, :, span(g)],
+            cs.at[g], cr.at[g], here.to_core,
+        )
+        sent.append(copy)
+        return copy
+
+    def first(g, copy):
+        copy.wait_recv()
+
+        def add(i, _):
+            j, zz, h = lax.div(i, 8), lax.rem(lax.div(i, 2), 4), lax.rem(i, 2)
+            G[j, zz, c, h, :, span(g)] = (
+                G[j, zz, c, h, :, span(g)].astype(f32) + Rc[j, zz, h, :, span(g)].astype(f32)
+            ).astype(low)
+            return 0
+
+        lax.fori_loop(0, 16, add, 0)
+        a = send(
+            G.at[:, 0:2, c, 1 - x, :, span(g)], A1.at[:, :, :, span(g)], a1s.at[g], a1r.at[g], here.to_x
+        )
+        b = send(
+            G.at[1 - y, 2:4, c, :, :, span(g)], B1.at[:, :, :, span(g)], b1s.at[g], b1r.at[g], here.to_y
+        )
+        sent.extend([a, b])
+        return a, b
+
+    def second(g, copies):
+        copies[0].wait_recv()
+
+        def add_a(i, _):
+            j, zz = lax.div(i, 2), lax.rem(i, 2)
+            G[j, zz, c, x, :, span(g)] = (
+                G[j, zz, c, x, :, span(g)].astype(f32) + A1[j, zz, :, span(g)].astype(f32)
+            ).astype(low)
+            return 0
+
+        lax.fori_loop(0, 4, add_a, 0)
+        a = send(
+            G.at[1 - y, 0:2, c, x, :, span(g)], A2.at[:, :, span(g)], a2s.at[g], a2r.at[g], here.to_y
+        )
+        copies[1].wait_recv()
+
+        def add_b(i, _):
+            zz, h = lax.div(i, 2), lax.rem(i, 2)
+            G[y, zz + 2, c, h, :, span(g)] = (
+                G[y, zz + 2, c, h, :, span(g)].astype(f32) + B1[zz, h, :, span(g)].astype(f32)
+            ).astype(low)
+            return 0
+
+        lax.fori_loop(0, 4, add_b, 0)
+        b = send(
+            G.at[y, 2:4, c, 1 - x, :, span(g)], B2.at[:, :, span(g)], b2s.at[g], b2r.at[g], here.to_x
+        )
+        sent.extend([a, b])
+        return a, b
+
+    def third(g, copies):
+        for number, (copy, part) in enumerate(zip(copies, (A2, B2))):
+            copy.wait_recv()
+
+            def add(i, _, number=number, part=part):
+                zz = 2 * number + i
+                G[y, zz, c, x, :, span(g)] = (
+                    G[y, zz, c, x, :, span(g)].astype(f32) + part[i, :, span(g)].astype(f32)
+                ).astype(low)
+                return 0
+
+            lax.fori_loop(0, 2, add, 0)
+        out = []
+        for step in (1, 2, 3):
+            out.append(
+                send(
+                    G.at[y, here.z_plus(step), c, x, :, span(g)], ZR.at[step - 1, :, span(g)],
+                    zs.at[g, step - 1], zr.at[g, step - 1], here.along(step),
+                )
+            )
+        sent.extend(out)
+        return out
+
+    def final(g, copies):
+        for copy in copies:
+            copy.wait_recv()
+        for b in range(4 * g, 4 * g + 4):
+            at = pl.ds(b * JCOLS, JCOLS)
+            total = G[y, z, c, x, :, at].astype(f32)
+            for step in range(3):
+                total = total + ZR[step, :, at].astype(f32)
+            F[b] = total.astype(low)
+
+    def spread(g):
+        at = pl.ds(4 * g, 4)
+        a = send(F.at[at], FX.at[at], fs.at[g, 0], fr.at[g, 0], here.to_x)
+        b = send(F.at[at], FY.at[at], fs.at[g, 1], fr.at[g, 1], here.to_y)
+        sent.extend([a, b])
+        return a, b
+
+    def put(g, table, h, j):
+        for b in range(4 * g, 4 * g + 4):
+            wg[h, :, cols(b * D + j * JCOLS, JCOLS)] = table[b].astype(f32)
+
+    def spread_on(g, copies):
+        a, b = copies
+        a.wait_recv()
+        at = pl.ds(4 * g, 2)
+        da = send(FX.at[at], FD.at[at], fs.at[g, 2], fr.at[g, 2], here.to_y)
+        b.wait_recv()
+        at = pl.ds(4 * g + 2, 2)
+        db = send(FY.at[at], FD.at[at], fs.at[g, 3], fr.at[g, 3], here.to_x)
+        sent.extend([da, db])
+        put(g, F, x, y)
+        put(g, FX, 1 - x, y)
+        put(g, FY, x, 1 - y)
+        return da, db
+
+    def spread_end(g, copies):
+        for copy in copies:
+            copy.wait_recv()
+        put(g, FD, 1 - x, 1 - y)
+
+    def token_send(table, landing, number):
+        out = []
+        for step in range(1, 8):
+            to = here.peer(step)
+            out.append(
+                send(table.at[to], landing.at[f], ts.at[number, step - 1], tr.at[number, step - 1], (r, to))
+            )
+        own = local(table.at[f], landing.at[f], ls.at[number])
+        sent.extend(out)
+        return out, own
+
+    def token_end(pair, landing, target):
+        for copy in pair[0]:
+            copy.wait_recv()
+        pair[1].wait()
+        hot = (outrow[...] == lax.broadcasted_iota(jnp.int32, (TOK_DEV, TOK_DEV), 1)).astype(f32).astype(low)
+        target[...] = jnp.dot(
+            hot, landing[...].reshape(TOK_DEV, D), preferred_element_type=f32
+        ).astype(low)
+
+    def narrow(target):
+        def one(i, _):
+            t, at = lax.div(i, 8), pl.ds(pl.multiple_of(lax.rem(i, 8) * 96, 96), 96)
+            target[t, at, :] = stg[t, at, :].astype(low)
+            return 0
+
+        lax.fori_loop(0, 16, one, 0)
+
+    c2 = c_send(2)
+    c1 = c_send(1)
+    c0 = c_send(0)
+    f2 = first(2, c2)
+    f1 = first(1, c1)
+    s2 = second(2, f2)
+    f0 = first(0, c0)
+    vec_copy.wait_recv()
+    vb[1] = vb[0] + vr[0]
+    vec_copy = send(vb.at[1], vr.at[1], vs.at[1], vrs.at[1], here.to_x)
+    sent.append(vec_copy)
+    ta_copies = token_send(rows_a, ta, 0)
+    s1 = second(1, f1)
+    t2 = third(2, s2)
+    for copy in stage:
+        copy.wait()
+    narrow(Lb)
+    stage = [local(root_r.at[t], stg.at[t], ks.at[2 + t]) for t in range(2)]
+    vec_copy.wait_recv()
+    vb[2] = vb[1] + vr[1]
+    vec_copy = send(vb.at[2], vr.at[2], vs.at[2], vrs.at[2], here.to_y)
+    sent.append(vec_copy)
+    s0 = second(0, f0)
+    t1 = third(1, s1)
+    final(2, t2)
+    e2 = spread(2)
+    for copy in stage:
+        copy.wait()
+    narrow(Rb)
+    vec_copy.wait_recv()
+    vb[3] = vb[2] + vr[2]
+    vec_copies = []
+    for step in (1, 2, 3):
+        vec_copies.append(
+            send(vb.at[3], vr.at[2 + step], vs.at[2 + step], vrs.at[2 + step], here.along(step))
+        )
+    sent.extend(vec_copies)
+    t0 = third(0, s0)
+    final(1, t1)
+    e1 = spread(1)
+    d2 = spread_on(2, e2)
+    final(0, t0)
+    jc = cols(y * JCOLS, JCOLS)
+    other = cols((1 - y) * JCOLS, JCOLS)
+    slot_copies = []
+    for step in range(1, 9):
+        to = here.peer(step)
+        for t in range(2):
+            b = block_of[2 * to + t]
+            flag = (b >= 0).astype(f32)
+            SO[step - 1, t] = (F[jnp.maximum(b, 0)].astype(f32) * flag).astype(low)
+        if step < 8:
+            slot_copies.append(
+                send(SO.at[step - 1], Gs.at[:, f, x, :, jc], ss.at[step - 1], sr.at[step - 1], (r, to))
+            )
+    sent.extend(slot_copies)
+    own = local(SO.at[7], Gs.at[:, f, x, :, jc], ls.at[2])
+    hops = []
+    for step in range(8):
+        src = lax.rem(f + 8 - step, 8)
+        if step == 0:
+            own.wait()
+        else:
+            slot_copies[step - 1].wait_recv()
+        part = Gs.at[:, src, x, :, jc]
+        hops.append(
+            (
+                send(part, part, ps.at[0, step], pr.at[0, step], here.to_x),
+                send(part, part, ps.at[1, step], pr.at[1, step], here.to_y),
+            )
+        )
+    ends = []
+    for step in range(8):
+        src = lax.rem(f + 8 - step, 8)
+        hops[step][0].wait_recv()
+        part = Gs.at[0, src, 1 - x, :, jc]
+        ends.append(send(part, part, ps.at[2, step], pr.at[2, step], here.to_y))
+        hops[step][1].wait_recv()
+        part = Gs.at[1, src, x, :, other]
+        ends.append(send(part, part, ps.at[3, step], pr.at[3, step], here.to_x))
+        sent.extend(hops[step])
+    sent.extend(ends)
+    e0 = spread(0)
+    d1 = spread_on(1, e1)
+    spread_end(2, d2)
+    token_end(ta_copies, ta, layer_out)
+    tb_copies = token_send(rows_b, tb, 1)
+    stage = [local(stat_l.at[0], stg.at[0], ks.at[4]), local(stat_r.at[0], stg.at[1], ks.at[5])]
+    for copy in ends:
+        copy.wait_recv()
+
+    def block(t):
+        return Gs[t].reshape(D, D)
+
+    for t in range(2):
+        whole = block(t)
+
+        def left(i, _, t=t, whole=whole):
+            at = pl.ds(pl.multiple_of(i * 192, 192), 192)
+            Rc[lax.div(i, 2), pl.ds(2 * lax.rem(i, 2), 2), :, :, :D] = (
+                jnp.dot(Lb[t, at, :], whole, preferred_element_type=f32)
+                .astype(low)
+                .reshape(2, 2, HALF, D)
+            )
+            return 0
+
+        lax.fori_loop(0, 4, left, 0)
+
+        def right(i, total, t=t):
+            at = pl.ds(pl.multiple_of(i * 192, 192), 192)
+            rows = Rc[lax.div(i, 2), pl.ds(2 * lax.rem(i, 2), 2), :, :, :D].reshape(192, D)
+            part = jnp.dot(rows, Rb[t], preferred_element_type=f32)
+            Pf[at, :] = part
+            return total + jnp.sum(part * part)
+
+        total = lax.fori_loop(0, 4, right, jnp.zeros((), f32))
+        scale = lax.rsqrt(jnp.full((1, 1), total * (1.0 / (D * D)) + RMS_EPS, f32))
+
+        def norm(i, _, t=t, scale=scale):
+            at = pl.ds(pl.multiple_of(i * 96, 96), 96)
+            Rc[t, lax.div(i, 2), :, :, cols(D + lax.rem(i, 2) * D, D)] = (
+                (Pf[at, :] * scale).astype(low).reshape(2, HALF, D)
+            )
+            return 0
+
+        lax.fori_loop(0, 8, norm, 0)
+
+    def update_part(to):
+        at = cols(D + lax.rem(to, 2) * D + y * JCOLS, JCOLS)
+        return Rc.at[:, lax.div(to, 2), x, :, at]
+
+    ucopies = []
+    for step in range(1, 8):
+        to = here.peer(step)
+        ucopies.append(
+            send(update_part(to), UL.at[pl.ds(2 * f, 2)], us.at[step - 1], ur.at[step - 1], (r, to))
+        )
+    sent.extend(ucopies)
+    own = local(update_part(f), UL.at[pl.ds(2 * f, 2)], ls.at[3])
+    outs = []
+    for t in range(2):
+        for copy in stage:
+            copy.wait()
+
+        def stat_left(i, _, t=t):
+            at = pl.ds(pl.multiple_of(i * 192, 192), 192)
+            rows = Gs[t, pl.ds(2 * i, 2)].reshape(192, D)
+            part = lax.dot_general(rows, block(t), (((1,), (1,)), ((), ())), preferred_element_type=f32)
+            stg[0, at, :] = STAT_DECAY * stg[0, at, :] + (1.0 - STAT_DECAY) * part
+            return 0
+
+        lax.fori_loop(0, 4, stat_left, 0)
+        outs = [local(stg.at[0], new_l.at[t], ks.at[8 + 2 * t])]
+        for i in range(3):
+            at = pl.ds(i * 256, 256)
+            strip = Gs[t, :, :, :, at].reshape(D, 256)
+            part = lax.dot_general(strip, block(t), (((0,), (0,)), ((), ())), preferred_element_type=f32)
+            stg[1, at, :] = STAT_DECAY * stg[1, at, :] + (1.0 - STAT_DECAY) * part
+        outs.append(local(stg.at[1], new_r.at[t], ks.at[9 + 2 * t]))
+        if t == 0:
+            for copy in outs:
+                copy.wait()
+            stage = [local(stat_l.at[1], stg.at[0], ks.at[6]), local(stat_r.at[1], stg.at[1], ks.at[7])]
+    d0 = spread_on(0, e0)
+    spread_end(1, d1)
+    for copy in ucopies:
+        copy.wait_recv()
+    own.wait()
+    for b in range(NBLK):
+        UN[b, x, :, jc] = UL[owner[b]]
+    part = UN.at[:, x, :, jc]
+    qa = send(part, part, qs.at[0], qr.at[0], here.to_x)
+    qb = send(part, part, qs.at[1], qr.at[1], here.to_y)
+    qa.wait_recv()
+    part = UN.at[0:6, 1 - x, :, jc]
+    qc = send(part, part, qs.at[2], qr.at[2], here.to_y)
+    qb.wait_recv()
+    part = UN.at[6:12, x, :, other]
+    qd = send(part, part, qs.at[3], qr.at[3], here.to_x)
+    sent.extend([qa, qb, qc, qd])
+    spread_end(0, d0)
+    total = vb[3]
+    for copy in vec_copies:
+        copy.wait_recv()
+    for step in range(3):
+        total = total + vr[3 + step]
+    tall = jnp.concatenate([total, jnp.zeros((112, D), f32)], axis=0)
+    vt[...] = jnp.transpose(tall)
+    grad = vt[pl.ds(pl.multiple_of(f * 96, 96), 96), :][:, :NBLK]
+    fresh1 = BETA_ONE * mom1[...] + (1.0 - BETA_ONE) * grad
+    fresh2 = BETA_TWO * mom2[...] + (1.0 - BETA_TWO) * grad * grad
+    out1[...] = fresh1
+    out2[...] = fresh2
+    outv[...] = vecs[...] - LR_VECTOR * (fresh1 / (1.0 - BETA_ONE**STEP)) / (
+        jnp.sqrt(fresh2 / (1.0 - BETA_TWO**STEP)) + ADAM_EPS
+    )
+    token_end(tb_copies, tb, input_grad)
+    qc.wait_recv()
+    qd.wait_recv()
+    for b in range(NBLK):
+        for h in range(2):
+            at = slice(b * D, (b + 1) * D)
+            nw[h, :, at] = wf[h, :, at] - LR_MATRIX * UN[b, h].astype(f32)
+    for copy in outs:
+        copy.wait()
+    for copy in sent:
+        copy.wait_send()
+
+
+def update_all(
+    block_of, owner, gq, go, gu, gd, vec, rows_a, rows_b, outrow, root_l, root_r, stat_l, stat_r, wf,
+    vecs, mom1, mom2,
+):
+    any_spec = pl.BlockSpec(memory_space=pl.ANY)
+    vmem = pl.BlockSpec(memory_space=pltpu.VMEM)
+    smem = pl.BlockSpec(memory_space=pltpu.SMEM)
+    dma = pltpu.SemaphoreType.DMA
+    shape = jax.ShapeDtypeStruct
+    low, f32 = jnp.bfloat16, jnp.float32
+    JW = 12 * JCOLS
+    split = lambda a: a.reshape(4, 2, 2, HALF, a.shape[1])
+    outs = pl.pallas_call(
+        update_kernel,
+        out_shape=[
+            shape((TOK_DEV, D), low), shape((TOK_DEV, D), low),
+            shape((2, HALF, 3 * GCOLS), f32), shape((2, HALF, 3 * GCOLS), f32),
+            shape((2, D, D), f32), shape((2, D, D), f32),
+            shape((96, NBLK), f32), shape((96, NBLK), f32), shape((96, NBLK), f32),
+        ],
+        in_specs=[smem, smem] + [any_spec] * 4 + [vmem] + [any_spec] * 2 + [vmem] + [any_spec] * 4 + [vmem] * 4,
+        out_specs=[vmem] * 4 + [any_spec] * 2 + [vmem] * 3,
+        scratch_shapes=[
+            pltpu.VMEM((2, 4, 2, 2, HALF, JW), low),
+            pltpu.VMEM((2, 4, 2, HALF, JW), low),
+            pltpu.VMEM((2, 2, HALF, JW), low),
+            pltpu.VMEM((2, HALF, JW), low),
+            pltpu.VMEM((2, 2, HALF, JW), low),
+            pltpu.VMEM((2, HALF, JW), low),
+            pltpu.VMEM((3, HALF, JW), low),
+            pltpu.VMEM((12, HALF, JCOLS), low),
+            pltpu.VMEM((12, HALF, JCOLS), low),
+            pltpu.VMEM((12, HALF, JCOLS), low),
+            pltpu.VMEM((12, HALF, JCOLS), low),
+            pltpu.VMEM((8, 2, HALF, JCOLS), low),
+            pltpu.VMEM((2, 8, 2, HALF, D), low),
+            pltpu.VMEM((2, D, D), low),
+            pltpu.VMEM((2, D, D), low),
+            pltpu.VMEM((2, D, D), f32),
+            pltpu.VMEM((D, D), f32),
+            pltpu.VMEM((16, HALF, JCOLS), low),
+            pltpu.VMEM((12, 2, HALF, D), low),
+            pltpu.VMEM((8, 64, D), low),
+            pltpu.VMEM((8, 64, D), low),
+            pltpu.VMEM((4, 16, D), f32),
+            pltpu.VMEM((6, 16, D), f32),
+            pltpu.VMEM((D, 128), f32),
+            dma((12, 2)), dma((3,)), dma((3,)),
+            dma((3,)), dma((3,)), dma((3,)), dma((3,)), dma((3,)), dma((3,)), dma((3,)), dma((3,)),
+            dma((3, 3)), dma((3, 3)), dma((3, 4)), dma((3, 4)),
+            dma((2, 7)), dma((2, 7)), dma((7,)), dma((7,)), dma((4, 8)), dma((4, 8)),
+            dma((7,)), dma((7,)), dma((4,)), dma((4,)), dma((6,)), dma((6,)), dma((4,)), dma((12,)),
+        ],
+        compiler_params=pltpu.CompilerParams(
+            collective_id=1, has_side_effects=True, vmem_limit_bytes=60 * MIB
+        ),
+        name="update_all",
+    )(
+        block_of, owner, split(gq), split(go), split(gu), split(gd), vec, rows_a, rows_b, outrow,
+        root_l, root_r, stat_l, stat_r, wf.reshape(2, HALF, 3 * GCOLS), vecs, mom1, mom2,
+    )
+    return outs
+
+
+def fast_body(
+    tokens,
+    cotangent,
+    place,
+    seq_lengths,
+    random_blocks,
+    owner_slot,
+    flat_weights,
+    vectors,
+    moment_first,
+    moment_second,
+    stat_left,
+    stat_right,
+    root_left,
+    root_right,
+):
+    peers = lax.axis_size("fsdp")
+    share_rows = TOK_DEV // peers
+    me = lax.axis_index("fsdp")
+    low = jnp.bfloat16
+    outrow = (place // TOK_DEV) * share_rows + place % TOK_DEV - me * share_rows
+    slot_ids = jnp.arange(TOK_DEV, dtype=jnp.int32)
+    hot = (slot_ids[:, None] == outrow[None, :]).astype(low)
+    tok_out = jnp.dot(hot, tokens, preferred_element_type=jnp.float32).astype(low)
+    cot_out = jnp.dot(hot, cotangent, preferred_element_type=jnp.float32).astype(low)
+    vec_pad = jnp.pad(vectors.astype(low), ((0, 0), (0, 128 - NBLK)))
+    w_attn, w_up, w_down, tok_in, cot_in, vec_in = gather_all(
+        tok_out.reshape(peers, share_rows, D),
+        cot_out.reshape(peers, share_rows, D),
+        flat_weights,
+        vec_pad,
+    )
+    w_attn = w_attn.reshape(D, 4 * D)
+    w_up = w_up.reshape(D, FF)
+    w_down = w_down.reshape(D, FF)
+    inputs = tok_in.reshape(TOK_DEV, D)
+    upstream = cot_in.reshape(TOK_DEV, D).astype(jnp.float32)
+    vecs_full = vec_in.reshape(D, 128)[:, :NBLK].astype(jnp.float32)
+    b_up = jnp.transpose(vecs_full[:, 8:]).reshape(FF)
+    seq_id, position, in_use, seq_blocks = layout(seq_lengths[0])
+    picks = random_keys(random_blocks, seq_blocks)
+    real_rows = in_use.astype(jnp.float32)[:, None]
+    bias_qkv = jnp.concatenate([vecs_full[:, 0], jnp.zeros((D,), jnp.float32), vecs_full[:, 1]])
+    qkv_low = (
+        jnp.dot(inputs, w_attn[:, : 3 * D], preferred_element_type=jnp.float32) + bias_qkv
+    ).astype(low)
+    qkv_heads = qkv_low.reshape(TOK_DEV, 3, H, HD)
+    queries = qkv_heads[:, 0]
+    key_heads = qkv_heads[:, 1]
+    value_heads = qkv_heads[:, 2]
+    score_scale = HD ** (-0.5)
+    keep_mask = allowed(
+        seq_id, position, in_use, picks, slot_ids, seq_id, position, in_use, slot_ids
+    )
+    scores = (
+        jnp.einsum("qhd,khd->hqk", queries, key_heads, preferred_element_type=jnp.float32)
+        * score_scale
+    )
+    scores = jnp.where(keep_mask, scores, MASKED_SCORE)
+    expo = jnp.exp(scores - jnp.max(scores, axis=-1, keepdims=True))
+    probs = expo / jnp.sum(expo, axis=-1, keepdims=True)
+    probs_low = probs.astype(low)
+    mixed = (
+        jnp.einsum("hqk,khd->qhd", probs_low, value_heads, preferred_element_type=jnp.float32)
+        .reshape(TOK_DEV, D)
+        .astype(low)
+    )
+    branch = (
+        jnp.dot(mixed, w_attn[:, 3 * D : 4 * D], preferred_element_type=jnp.float32)
+        + vecs_full[:, 2]
+    )
+    hidden_one = inputs.astype(jnp.float32) + branch
+    x_one, norm_one_back = jax.vjp(layer_norm, hidden_one, vecs_full[:, 4], vecs_full[:, 5])
+    x_one_low = x_one.astype(low)
+    pre_act = jnp.dot(x_one_low, w_up, preferred_element_type=jnp.float32) + b_up
+    act, gelu_back = jax.vjp(gelu_tanh, pre_act)
+    act_low = act.astype(low)
+    ffn = contract_cols(act_low, w_down) + vecs_full[:, 3]
+    hidden_two = x_one + ffn
+    result, norm_two_back = jax.vjp(layer_norm, hidden_two, vecs_full[:, 6], vecs_full[:, 7])
+    layer_rows = (result * real_rows).astype(low)
+    d_result = upstream * real_rows
+    d_two, d_gain_two, d_shift_two = norm_two_back(d_result)
+    d_ffn = d_two.astype(low)
+    d_act = jnp.dot(d_ffn, w_down, preferred_element_type=jnp.float32)
+    (d_pre,) = gelu_back(d_act)
+    d_pre_low = d_pre.astype(low)
+    grad_down = contract_rows(d_ffn, act_low).astype(low)
+    grad_up = contract_rows(x_one_low, d_pre_low).astype(low)
+    d_x_one = d_two + contract_cols(d_pre_low, w_up)
+    d_one, d_gain_one, d_shift_one = norm_one_back(d_x_one)
+    d_branch = d_one.astype(low)
+    grad_out = contract_rows(mixed, d_branch).astype(low)
+    d_mixed = contract_cols(d_branch, w_attn[:, 3 * D : 4 * D]).astype(low).reshape(TOK_DEV, H, HD)
+    prob_grad = jnp.einsum("qhd,khd->hqk", d_mixed, value_heads, preferred_element_type=jnp.float32)
+    score_grad = (
+        probs * (prob_grad - jnp.sum(probs * prob_grad, axis=-1, keepdims=True))
+    ).astype(low)
+    value_grad = jnp.einsum("hqk,qhd->khd", probs_low, d_mixed, preferred_element_type=jnp.float32)
+    query_grad = (
+        jnp.einsum("hqk,khd->qhd", score_grad, key_heads, preferred_element_type=jnp.float32)
+        * score_scale
+    )
+    key_grad = (
+        jnp.einsum("hqk,qhd->khd", score_grad, queries, preferred_element_type=jnp.float32)
+        * score_scale
+    )
+    d_qkv = jnp.concatenate(
+        [
+            query_grad.reshape(TOK_DEV, D),
+            key_grad.reshape(TOK_DEV, D),
+            value_grad.reshape(TOK_DEV, D),
+        ],
+        axis=1,
+    ).astype(low)
+    grad_qkv = contract_rows(inputs, d_qkv).astype(low)
+    d_inputs = d_one + contract_cols(d_qkv, w_attn[:, : 3 * D])
+    grad_rows = d_inputs.astype(low)
+    qkv_sums = jnp.sum(d_qkv.astype(jnp.float32), axis=0)
+    up_sums = jnp.sum(d_pre_low.astype(jnp.float32), axis=0).reshape(FF // D, D)
+    vec_grad = jnp.concatenate(
+        [
+            qkv_sums[None, :D],
+            qkv_sums[None, 2 * D :],
+            jnp.sum(d_branch.astype(jnp.float32), axis=0)[None],
+            jnp.sum(d_ffn.astype(jnp.float32), axis=0)[None],
+            d_gain_one[None],
+            d_shift_one[None],
+            d_gain_two[None],
+            d_shift_two[None],
+            up_sums,
+            jnp.zeros((4, D), jnp.float32),
+        ],
+        axis=0,
+    )
+    slots = jnp.arange(16, dtype=jnp.int32)
+    hits = slots[:, None] == owner_slot[None, :]
+    block_of = jnp.sum(jnp.where(hits, jnp.arange(NBLK, dtype=jnp.int32)[None, :] + 1, 0), axis=1) - 1
+    outs = update_all(
+        block_of.astype(jnp.int32),
+        owner_slot,
+        grad_qkv,
+        grad_out,
+        grad_up,
+        grad_down,
+        vec_grad,
+        layer_rows.reshape(peers, share_rows, D),
+        grad_rows.reshape(peers, share_rows, D),
+        outrow[:, None],
+        root_left,
+        root_right,
+        stat_left,
+        stat_right,
+        flat_weights,
+        vectors,
+        moment_first,
+        moment_second,
+    )
+    layer_out, input_grad, weight_grads, new_weights, *others = outs
+    return (
+        layer_out,
+        input_grad,
+        weight_grads.reshape(96, NBLK * D),
+        new_weights.reshape(96, NBLK * D),
+        *others,
+    )
+
+
+def plain_body(
     tokens,
     cotangent,
     place,
@@ -388,4 +1216,6 @@
         P("fsdp", None),
         P("fsdp", None),
     )
+    shaped = mesh.shape["fsdp"] == 8 and mesh.shape["rep"] == 4
+    body = fast_body if shaped else plain_body
     return jax.shard_map(body, mesh=mesh, in_specs=in_specs, out_specs=out_specs, check_vma=False)

time: 874 us -> 449 us (0.51)
  waiting for transfers between devices: 473 us -> 0 us
  Pallas kernels: 0 us -> 259 us
  blocking collectives: 125 us -> 0 us
  starting transfers between devices: 33.3 us -> 0 us
  matrix products: 129 us -> 100 us
  other arithmetic: 54.6 us -> 35.5 us
  between operations: 15.1 us -> 1.64 us
    reduce_scatter x2 -> x0, waiting for transfers between devices: 311 us -> none  [the longest x1 279 us: body(): lax.psum_scatter(jnp.concatenate([attn_mats, ffn_mats], axis=1), 'fsdp',...]
    pallas_call x0 -> x2, Pallas kernels: none -> 259 us  [the longest x1 173 us: update_all(): pl.pallas_call(update_kernel, out_shape=[shape((TOK_DEV, D), low), shape(...]
    all_gather x2 -> x0, waiting for transfers between devices: 121 us -> none  [the longest x1 86.7 us: body(): lax.all_gather(flat_weights.astype(jnp.bfloat16), 'fsdp', axis=0, tiled=T...]
    all_to_all x1 -> x0, blocking collectives: 57 us -> none  [body(): lax.all_to_all(outbound.astype(jnp.bfloat16), 'fsdp', split_axis=1, conca...]
    all_gather x1 -> x0, blocking collectives: 47.1 us -> none  [body(): lax.all_gather(vectors.astype(jnp.bfloat16), 'fsdp', axis=0, tiled=True)]
    all_to_all x5 -> x0, starting transfers between devices: 32.9 us -> none  [the longest x1 8.04 us: body(): lax.all_to_all(grad_rows.reshape(peers, share_rows, D), 'fsdp', split_axi...]
    unnamed x6 -> x0, waiting for transfers between devices: 28.4 us -> none
    unnamed x101 -> x73, local copies, waits for them, and re-layouts: 12 us -> 36.2 us
  transfers between devices with their start and end apart: 10 -> 0, of which waited for: 6 -> 0; matrix products, arithmetic and copies ran while one was open for 13% -> 0% of each run, Pallas kernels for 0% -> 0%
where the time goes in v1:
time: 449 us; the launch traced here: 441 us
  Pallas kernels  259 us (58%)
  matrix products  100 us (22%)
  local copies, waits for them, and re-layouts  44.6 us (10%)
  other arithmetic  35.5 us (8%)
    pallas_call x1, Pallas kernels, update_all(): pl.pallas_call(update_kernel, out_shape=[shape((TOK_DEV, D), low), shape(...  173 us
    pallas_call x1, Pallas kernels, gather_all(): pl.pallas_call(gather_kernel, out_shape=[shape((4, 2, 2, HALF, GCOLS), lo...  85.7 us
    unnamed x73, local copies, waits for them, and re-layouts  36.2 us
    dot_general x4, matrix products, contract_rows(): lax.dot_general(left, right, (((0,), (0,)), ((), ())), preferred_element_...  16.6 us
    sub x1, other arithmetic, fast_body(): expo = jnp.exp(scores - jnp.max(scores, axis=-1, keepdims=True))  15.1 us
    dot_general x4, matrix products, contract_cols(): lax.dot_general(left, right, (((1,), (1,)), ((), ())), preferred_element_...  13.5 us
    dot_general x1, matrix products, fast_body(): jnp.einsum('hqk,qhd->khd', probs_low, d_mixed, preferred_element_type=jnp...  12.5 us
    dot_general x1, matrix products, fast_body(): jnp.einsum('hqk,khd->qhd', probs_low, value_heads, preferred_element_type...  12.3 us

profile of v1, /device:TPU:9, one launch (start us, length us, event | category | flops | bytes accessed | tf_op | source)
XLA Modules:
  0.0 441.0 jit_solution(10858492499450929228)
XLA Ops:
  6.2 0.9 add_select_fusion
  7.3 1.4 copy.99.mom1
  8.7 1.4 copy.100.mom2
  10.2 1.4 copy.98.vecs
  14.2 1.7 convolution_convert_fusion.6
  15.9 85.7 %gather_all.1 = (bf16[4,2,2,48,3072]{4,3,2,1,0:T(8,128)(2,1)S(1)}, bf16[4,2,2,48,3072]{4,3,2,1,0:T(8,128)(2,1)S(1)}, bf16[4,2,2,48,3072]{4,3,2,1,0:T(8,128)(2,1)...) custom-call(bf16[8,64,768]{2,1,0:T(8,128)(2,1)S(1)} %bitcast.120, ...), custom_call_target="tpu_custom_call" | custom-call | tf_op jit(solution)/shard_map/gather_all/pallas_call | solution.py:268
  101.6 2.2 copy-done.3
  103.8 2.2 copy-done.4
  105.9 2.1 copy-done.5
  108.6 5.4 %fusion.8 = bf16[512,2304]{1,0:T(8,128)(2,1)} fusion(bf16[512,768]{1,0:T(8,128)(2,1)S(1)} %bitcast.136, bf16[768,3072]{1,0:T(8,128)(2,1)} %bitcast.122, f32[2304]{0:T(1024)S(1)} %pad_maximum_fusion.1), kind=kOutput, calls=%fused_computation.22 | convolution fusion | flops 1814298624 | bytes 6693888 | tf_op jit(solution)/shard_map/dot_general | solution.py:796
  114.0 4.3 copy.90
  118.3 9.7 %multiply_select_fusion = f32[12,512,512]{1,2,0:T(8,128)} fusion(s32[12,512]{1,0:T(8,128)S(1)} %get-tuple-element.118, s32[12,512]{1,0:T(8,128)S(1)} %get-tuple-element.119, s32[12,512]{1,0:T(8,128)S(1)} %get-tuple-element.117, s32[512]{0:T(512)S(1)} %get-tuple-element.125, pred[512,512]{0,1:T(8,128)(4,1)S(1)} %fusion.28, ...), kind=kOutput, calls=%fused_computation.4 | convolution fusion | flops 434110464 | bytes 15017984 | tf_op jit(solution)/shard_map/qhd,khd->hqk/dot_general | solution.py:807
  128.0 15.1 %fusion.59 = (f32[12,512]{1,0:T(8,128)S(1)}, f32[12,512,512]{1,2,0:T(8,128)}) fusion(f32[12,512,512]{1,2,0:T(8,128)} %multiply_select_fusion), kind=kOutput, calls=%fused_computation.158 | output fusion | flops 6291967 | bytes 25190400 | tf_op jit(solution)/shard_map/sub | solution.py:811
  143.1 12.3 %fusion.19 = bf16[12,64,512]{2,1,0:T(8,128)(2,1)} fusion(bf16[512,3,12,64]{0,3,2,1:T(8,128)(2,1)} %bitcast.142, f32[12,512]{1,0:T(8,128)S(1)} %get-tuple-element.126, f32[12,512,512]{1,2,0:T(8,128)} %multiply_select_fusion), kind=kOutput, calls=%fused_computation.56 | convolution fusion | flops 412490240 | bytes 26763264 | tf_op jit(solution)/shard_map/hqk,khd->qhd/dot_general | solution.py:815
  155.5 2.4 fusion.60
  158.2 5.3 %fusion.51 = f32[512,3072]{1,0:T(8,128)S(1)} fusion(bf16[768,3072]{1,0:T(8,128)(2,1)} %bitcast.128, f32[512,768]{1,0:T(8,128)S(1)} %get-tuple-element.129, f32[768]{0:T(1024)S(1)} %get-tuple-element.91, f32[768]{0:T(1024)S(1)} %get-tuple-element.92, f32[512]{0:T(512)S(1)} %fusion.46, f32[512]{0:T(512)S(1)} %broadcast_multiply_fusion.1), kind=kOutput, calls=%fused_computation.153 | convolution fusion | flops 2417885184 | bytes 12593152 | tf_op jit(solution)/shard_map/dot_general | solution.py:826
  163.5 4.2 fusion.61
  168.9 1.7 fusion.55
  170.8 6.7 %convert_reduce_fusion = (f32[3072]{0:T(1024)S(1)}, bf16[512,3072]{1,0:T(8,128)(2,1)S(1)}) fusion(f32[512,3072]{1,0:T(8,128)S(1)} %fusion.51, f32[3072]{0:T(1024)S(1)} %add.194, bf16[512,768]{1,0:T(8,128)(2,1)S(1)} %get-tuple-element.103, bf16[768,3072]{1,0:T(8,128)(2,1)S(1)} %bitcast.135), kind=kOutput, calls=%fused_computation.14 | convolution fusion | flops 2452091904 | bytes 14966784 | tf_op jit(solution)/shard_map/dot_general | solution.py:836
  177.5 4.8 %convolution_convert_fusion = bf16[768,3072]{1,0:T(8,128)(2,1)} fusion(bf16[512,768]{1,0:T(8,128)(2,1)S(1)} %get-tuple-element.103, f32[512,3072]{1,0:T(8,128)S(1)} %fusion.51, f32[3072]{0:T(1024)S(1)} %add.194), kind=kOutput, calls=%fused_computation.17 | convolution fusion | flops 2434007040 | bytes 11808768 | tf_op jit(solution)/shard_map/dot_general | solution.py:85
  182.4 4.2 multiply_reduce_fusion.3
  186.6 2.1 fusion.54
  188.9 4.8 %convolution_convert_fusion.1 = bf16[768,3072]{1,0:T(8,128)(2,1)} fusion(bf16[512,3072]{1,0:T(8,128)(2,1)S(1)} %copy-done.16, f32[512,768]{1,0:T(8,128)S(1)} %get-tuple-element.129, f32[768]{0:T(1024)S(1)} %get-tuple-element.91, f32[768]{0:T(1024)S(1)} %get-tuple-element.92, f32[512]{0:T(512)S(1)} %fusion.46, f32[512]{0:T(512)S(1)} %broadcast_multiply_fusion.1), kind=kOutput, calls=%fused_computation.18 | convolution fusion | flops 2420244480 | bytes 9447424 | tf_op jit(solution)/shard_map/dot_general | solution.py:85
  194.0 1.8 convolution_convert_fusion.3
  195.8 2.1 convolution_convert_fusion.4
  197.9 1.2 copy.93
  199.0 12.5 %fusion.22 = bf16[12,64,512]{2,1,0:T(8,128)(2,1)} fusion(bf16[512,12,64]{0,2,1:T(8,128)(2,1)} %bitcast.163, f32[12,512]{1,0:T(8,128)S(1)} %get-tuple-element.126, f32[12,512,512]{1,2,0:T(8,128)} %multiply_select_fusion), kind=kOutput, calls=%fused_computation.57 | convolution fusion | flops 412490240 | bytes 14180352 | tf_op jit(solution)/shard_map/hqk,qhd->khd/dot_general | solution.py:850
  211.5 10.4 %multiply_reduce_fusion = (f32[12,512]{1,0:T(8,128)S(1)}, f32[12,512,512]{1,2,0:T(8,128)}) fusion(f32[12,512,512]{1,2,0:T(8,128)} %get-tuple-element.127, f32[12,512]{1,0:T(8,128)S(1)} %get-tuple-element.126, bf16[512,12,64]{0,2,1:T(8,128)(2,1)} %bitcast.164, bf16[512,3,12,64]{0,3,2,1:T(8,128)(2,1)S(1)} %bitcast.143), kind=kOutput, calls=%fused_computation.2 | convolution fusion | flops 412084224 | bytes 26796032 | tf_op jit(solution)/shard_map/qhd,khd->hqk/dot_general | solution.py:846
  221.9 1.2 slice-done.7
  223.2 1.2 slice-done.8
  224.4 6.9 %multiply_convert_fusion = bf16[12,512,512]{1,2,0:T(8,128)(2,1)S(1)} fusion(f32[12,512,512]{1,2,0:T(8,128)} %get-tuple-element.134, f32[12,512]{1,0:T(8,128)S(1)} %get-tuple-element.133, f32[12,512,512]{1,2,0:T(8,128)S(1)} %bitcast.140, f32[12,512]{1,0:T(8,128)S(1)} %get-tuple-element.126), kind=kLoop, calls=%fused_computation.1 | loop fusion | flops 12582912 | bytes 31506432 | tf_op jit(solution)/shard_map/convert_element_type | solution.py:849
  231.3 2.0 multiply_convert_fusion.3
  233.4 1.1 multiply_convert_fusion.4
  234.5 1.6 slice-done.1
  236.8 3.0 add_convert_fusion
  240.2 1.3 concatenate.12.vec
  241.4 5.2 %convolution_convert_fusion.2 = bf16[768,2304]{1,0:T(8,128)(2,1)} fusion(bf16[512,768]{1,0:T(8,128)(2,1)S(1)} %bitcast.138, bf16[512,768]{0,1:T(8,128)(2,1)S(1)} %bitcast.167, bf16[512,768]{0,1:T(8,128)(2,1)} %bitcast.160, bf16[512,768]{0,1:T(8,128)(2,1)} %bitcast.148), kind=kOutput, calls=%fused_computation.19 | convolution fusion | flops 1820786688 | bytes 6684672 | tf_op jit(solution)/shard_map/dot_general | solution.py:85
  246.7 173.5 %update_all.1 = (bf16[512,768]{1,0:T(8,128)(2,1)}, bf16[512,768]{1,0:T(8,128)(2,1)}, f32[2,48,9216]{2,1,0:T(8,128)}, f32[2,48,9216]{2,1,0:T(8,128)}, f32[2,768,7...) custom-call(s32[16]{0:T(128)} %broadcast_add_fusion.block_of, ...), custom_call_target="tpu_custom_call" | custom-call | tf_op jit(solution)/shard_map/update_all/pallas_call | solution.py:700
  420.1 1.5 copy.101
  421.6 1.5 copy.102
  423.1 1.5 copy.103
  424.6 2.1 copy.115
  426.6 2.2 copy.116
  428.8 4.2 copy.117
  433.0 1.8 copy.118
  434.8 2.4 copy.119
  437.2 0.9 slice-done.9
  438.4 2.2 copy.120
  (121 shorter events, 12.1 us)
Async XLA Ops:
  0.6 12.9 %copy-start = (bf16[512,768]{1,0:T(8,128)(2,1)S(1)}, bf16[512,768]{1,0:T(8,128)(2,1)}, u32[]{:S(2)}) copy-start(bf16[512,768]{1,0:T(8,128)(2,1)} %param.15) | copy-start | bytes 2359300
  12.7 3.1 copy-start.2
  101.6 2.2 copy-start.3
  103.8 2.2 copy-start.4
  105.9 2.1 copy-start.5
  157.9 5.6 %slice-start.4 = ((s8[4718592]{0:T(1024)(128)(4,1)}), s8[4194304]{0:T(1024)(128)(4,1)S(1)}, s32[]{:S(2)}) async-start(s8[4718592]{0:T(1024)(128)(4,1)} %bitcast.132), calls=%async_computation.4 | async-start | bytes 8388608
  158.2 5.3 %slice-start.5 = ((s8[4718592]{0:T(1024)(128)(4,1)}), s8[524288]{0:T(1024)(128)(4,1)S(1)}, s32[]{:S(2)}) async-start(s8[4718592]{0:T(1024)(128)(4,1)} %bitcast.132), calls=%async_computation.5 | async-start | bytes 1048576
  168.9 13.5 %slice-start.2 = ((s8[4718592]{0:T(1024)(128)(4,1)}), s8[4194304]{0:T(1024)(128)(4,1)S(1)}, s32[]{:S(2)}) async-start(s8[4718592]{0:T(1024)(128)(4,1)} %bitcast.129), calls=%async_computation.2 | async-start | bytes 8388608
  170.8 11.6 %slice-start.3 = ((s8[4718592]{0:T(1024)(128)(4,1)}), s8[524288]{0:T(1024)(128)(4,1)S(1)}, s32[]{:S(2)}) async-start(s8[4718592]{0:T(1024)(128)(4,1)} %bitcast.129), calls=%async_computation.3 | async-start | bytes 1048576
  177.5 4.9 %copy-start.15 = (bf16[512,3072]{1,0:T(8,128)(2,1)}, bf16[512,3072]{1,0:T(8,128)(2,1)S(1)}, u32[]{:S(2)}) copy-start(bf16[512,3072]{1,0:T(8,128)(2,1)S(1)} %get-tuple-element.101) | copy-start | bytes 9437188
  186.6 2.4 copy-start.16
  188.9 4.8 %copy-start.8 = (f32[512,768]{1,0:T(8,128)}, f32[512,768]{1,0:T(8,128)S(1)}, u32[]{:S(2)}) copy-start(f32[512,768]{1,0:T(8,128)S(1)} %get-tuple-element.107) | copy-start | bytes 4718596
  188.9 5.0 %copy-start.14 = (bf16[12,64,512]{2,1,0:T(8,128)(2,1)S(1)}, bf16[12,64,512]{2,1,0:T(8,128)(2,1)}, u32[]{:S(2)}) copy-start(bf16[12,64,512]{2,1,0:T(8,128)(2,1)} %fusion.19) | copy-start | bytes 2359300
  199.0 12.5 %copy-start.6 = (bf16[512,2304]{0,1:T(8,128)(2,1)S(1)}, bf16[512,2304]{0,1:T(8,128)(2,1)}, u32[]{:S(2)}) copy-start(bf16[512,2304]{0,1:T(8,128)(2,1)} %copy.90) | copy-start | bytes 7077892
  211.5 10.4 %slice-start.6 = ((s8[12582912]{0:T(1024)(128)(4,1)}), s8[4194304]{0:T(1024)(128)(4,1)S(1)}, s32[]{:S(2)}) async-start(s8[12582912]{0:T(1024)(128)(4,1)} %bitcast.139), calls=%async_computation.6 | async-start | bytes 8388608
  211.5 11.6 %slice-start.7 = ((s8[12582912]{0:T(1024)(128)(4,1)}), s8[4194304]{0:T(1024)(128)(4,1)S(1)}, s32[]{:S(2)}) async-start(s8[12582912]{0:T(1024)(128)(4,1)} %bitcast.139), calls=%async_computation.7 | async-start | bytes 8388608
  211.5 12.8 %slice-start.8 = ((s8[12582912]{0:T(1024)(128)(4,1)}), s8[4194304]{0:T(1024)(128)(4,1)S(1)}, s32[]{:S(2)}) async-start(s8[12582912]{0:T(1024)(128)(4,1)} %bitcast.139), calls=%async_computation.8 | async-start | bytes 8388608
  231.3 3.2 slice-start
  233.3 6.4 %copy-start.11 = (bf16[12,64,512]{2,1,0:T(8,128)(2,1)}, bf16[12,64,512]{2,1,0:T(8,128)(2,1)S(1)}, u32[]{:S(2)}) copy-start(bf16[12,64,512]{2,1,0:T(8,128)(2,1)S(1)} %multiply_convert_fusion.3) | copy-start | bytes 2359300
  233.3 2.8 slice-start.1
  233.3 3.2 copy-start.9
  233.3 3.4 copy-start.12
  234.5 5.3 %copy-start.7 = (bf16[12,64,512]{2,1,0:T(8,128)(2,1)}, bf16[12,64,512]{2,1,0:T(8,128)(2,1)S(1)}, u32[]{:S(2)}) copy-start(bf16[12,64,512]{2,1,0:T(8,128)(2,1)S(1)} %multiply_convert_fusion.4) | copy-start | bytes 2359300
  236.7 4.7 %copy-start.13 = (bf16[12,64,512]{2,1,0:T(8,128)(2,1)S(1)}, bf16[12,64,512]{2,1,0:T(8,128)(2,1)}, u32[]{:S(2)}) copy-start(bf16[12,64,512]{2,1,0:T(8,128)(2,1)} %fusion.22) | copy-start | bytes 2359300
  426.6 8.2 %slice-start.11 = ((s8[4718592]{0:T(1024)(128)(4,1)}), s8[4194304]{0:T(1024)(128)(4,1)S(1)}, s32[]{:S(2)}) async-start(s8[4718592]{0:T(1024)(128)(4,1)} %bitcast.151), calls=%async_computation.11 | async-start | bytes 8388608
  428.8 4.2 copy-start.10
  428.8 6.0 %slice-start.12 = ((s8[4718592]{0:T(1024)(128)(4,1)}), s8[524288]{0:T(1024)(128)(4,1)S(1)}, s32[]{:S(2)}) async-start(s8[4718592]{0:T(1024)(128)(4,1)} %bitcast.151), calls=%async_computation.12 | async-start | bytes 1048576
  433.0 5.2 %slice-start.9 = ((s8[4718592]{0:T(1024)(128)(4,1)}), s8[4194304]{0:T(1024)(128)(4,1)S(1)}, s32[]{:S(2)}) async-start(s8[4718592]{0:T(1024)(128)(4,1)} %bitcast.149), calls=%async_computation.9 | async-start | bytes 8388608
  434.8 3.6 slice-start.10
  434.8 5.8 %copy-start.1 = (bf16[512,768]{1,0:T(8,128)(2,1)S(1)}, bf16[512,768]{1,0:T(8,128)(2,1)}, u32[]{:S(2)}) copy-start(bf16[512,768]{1,0:T(8,128)(2,1)} %param.15) | copy-start | bytes 2359300

commit v2 on v0

--- a/solution.py
+++ b/solution.py
@@ -1,6 +1,10 @@
+import functools
+
 import jax
 import jax.numpy as jnp
 from jax import lax
+from jax.experimental import pallas as pl
+from jax.experimental.pallas import tpu as pltpu
 from jax.sharding import PartitionSpec as P
 
 D = 768
@@ -89,7 +93,1218 @@
     )
 
 
-def body(
+MESH = pl.DeviceIdType.MESH
+HALF = 48
+GCOLS = 3072
+JCOLS = 384
+MIB = 2**20
+
+
+class Here:
+    def __init__(self, corner=False):
+        r, f = lax.axis_index("rep"), lax.axis_index("fsdp")
+        self.r, self.f = r, f
+        self.x, self.y = lax.rem(r, 2), lax.div(r, 2)
+        self.z, self.c = lax.div(f, 2), lax.rem(f, 2)
+        self.to_x = (r + 1 - 2 * self.x, f)
+        self.to_y = (r + 2 - 4 * self.y, f)
+        self.to_d = (3 - r, f)
+        self.corner = corner
+        self.to_core = (r, f + 1 - 2 * self.c)
+
+    def z_plus(self, step):
+        return lax.rem(self.z + step, 4)
+
+    def along(self, step):
+        return (self.r, 2 * self.z_plus(step) + self.c)
+
+    def peer(self, step):
+        return lax.rem(self.f + step, 8)
+
+    def greet(self):
+        barrier = pltpu.get_barrier_semaphore()
+        friends = [self.to_x, self.to_y] + [self.to_d] * self.corner
+        friends += [(self.r, self.peer(s)) for s in range(1, 8)]
+        for friend in friends:
+            pl.semaphore_signal(barrier, inc=1, device_id=friend, device_id_type=MESH)
+        return lambda: pl.semaphore_wait(barrier, len(friends))
+
+
+def send(src, dst, send_sem, recv_sem, device):
+    copy = pltpu.make_async_remote_copy(
+        src_ref=src,
+        dst_ref=dst,
+        send_sem=send_sem,
+        recv_sem=recv_sem,
+        device_id=device,
+        device_id_type=MESH,
+    )
+    copy.start()
+    return copy
+
+
+def local(src, dst, sem):
+    copy = pltpu.make_async_copy(src, dst, sem)
+    copy.start()
+    return copy
+
+
+def cols(start, width):
+    return pl.ds(pl.multiple_of(start, 128), width)
+
+
+def forward_kernel(
+    outrow, tok, cot, wf, vec, bias, use, use_row, root_l, root_r,
+    o0, o1, o2, o_vt, o_x, o_cot, o_qkv, o_p, o_mix, o_n1, o_r1, o_u, o_f, o_dg, o_n2, o_r2, o_y, o_root,
+    w0, w1, w2, tok_in, cot_in, vec_in, tok_s, cot_s,
+    vt, qkv, P, mix, n1, r1, x1, u, fa, dg, n2, r2, yo, xT, mT, uT, feat, stg, rb,
+    wl, zs, zr, xs, xr, ys, yr, ds, dr, cs, cr, ls, ts, tr, os, ks,
+):
+    low, f32 = jnp.bfloat16, jnp.float32
+    here = Here()
+    wait_all = here.greet()
+    x, y, z, c, f = here.x, here.y, here.z, here.c, here.f
+    whole = [w0, w1, w2]
+    whole_out = [o0, o1, o2]
+    wide = GCOLS // 2
+    sent = []
+    outs = []
+    count = [0]
+
+    def keep(src, dst):
+        outs.append(local(src, dst, os.at[count[0]]))
+        count[0] += 1
+
+    def narrow(g):
+        def one(i, _):
+            h, part = lax.div(i, 4), lax.rem(i, 4)
+            at = cols(g * GCOLS + part * D, D)
+            wl[h, :, at] = wf[h, :, at].astype(low)
+            return 0
+
+        lax.fori_loop(0, 8, one, 0)
+        return local(wl.at[:, :, g * GCOLS : (g + 1) * GCOLS], whole[g].at[z, c], ls.at[g])
+
+    def z_send(g):
+        out = []
+        for step in (1, 2, 3):
+            out.append(
+                send(
+                    wl.at[x, :, cols(g * GCOLS + y * wide, wide)],
+                    whole[g].at[z, c, x, :, cols(y * wide, wide)],
+                    zs.at[g, step - 1],
+                    zr.at[g, step - 1],
+                    here.along(step),
+                )
+            )
+        sent.extend(out)
+        return out
+
+    def rows_out(table, landing, number):
+        out = []
+        for step in range(1, 8):
+            to = here.peer(step)
+            src = table if number == 2 else table.at[to]
+            out.append(
+                send(src, landing.at[f], ts.at[number, step - 1], tr.at[number, step - 1], (here.r, to))
+            )
+        sent.extend(out)
+        return out
+
+    def plane(g, copies):
+        out = []
+        for step in (1, 2, 3):
+            copies[step - 1].wait_recv()
+            src = lax.rem(z + 4 - step, 4)
+            part = whole[g].at[src, c, x, :, cols(y * wide, wide)]
+            xc = send(part, part, xs.at[g, step - 1], xr.at[g, step - 1], here.to_x)
+            yc = send(part, part, ys.at[g, step - 1], yr.at[g, step - 1], here.to_y)
+            out.append((xc, yc))
+            sent.extend([xc, yc])
+        core(g, 0, x, y)
+        return out
+
+    cores = {0: [], 1: [], 2: []}
+
+    def core(g, number, h, j):
+        part = whole[g].at[:, c, h, :, cols(j * wide, wide)]
+        copy = send(part, part, cs.at[g, number], cr.at[g, number], here.to_core)
+        sent.append(copy)
+        cores[g].append(copy)
+
+    def turn(g, copies):
+        out = []
+        for step in (1, 2, 3):
+            src = lax.rem(z + 4 - step, 4)
+            xc, yc = copies[step - 1]
+            xc.wait_recv()
+            part = whole[g].at[src, c, 1 - x, :, cols(y * wide, wide // 2)]
+            out.append(send(part, part, ds.at[g, 0, step - 1], dr.at[g, 0, step - 1], here.to_y))
+            yc.wait_recv()
+            part = whole[g].at[src, c, x, :, cols((1 - y) * wide + wide // 2, wide // 2)]
+            out.append(send(part, part, ds.at[g, 1, step - 1], dr.at[g, 1, step - 1], here.to_x))
+        sent.extend(out)
+        core(g, 1, 1 - x, y)
+        core(g, 2, x, 1 - y)
+        return out
+
+    def last(g, copies):
+        for copy in copies:
+            copy.wait_recv()
+        core(g, 3, 1 - x, 1 - y)
+
+    def ready(g):
+        for copy in cores[g]:
+            copy.wait_recv()
+        keep(whole[g], whole_out[g])
+
+    def square(ref, at):
+        return ref[:, :, :, :, at].reshape(D, at.size)
+
+    def order(source, target):
+        hot = (lax.broadcasted_iota(jnp.int32, (TOK_DEV, TOK_DEV), 0) == outrow[...]).astype(f32).astype(low)
+        target[...] = jnp.dot(hot, source[...], preferred_element_type=f32).astype(low).reshape(8, 64, D)
+
+    def project():
+        for part in range(3):
+
+            def one(i, _, part=part):
+                at = cols(i * 256, 256)
+                to = cols(part * D + i * 256, 256)
+                acc = jnp.dot(tok_in[...].reshape(TOK_DEV, D), square(w0, to), preferred_element_type=f32)
+                if part == 0:
+                    acc = (acc + vt[0:1, at]) * (HD ** (-0.5))
+                if part == 2:
+                    acc = acc + vt[1:2, at]
+                qkv[:, to] = acc.astype(low)
+                return 0
+
+            lax.fori_loop(0, 3, one, 0)
+
+    def features():
+        def one(i, _):
+            gap = jnp.zeros((BLK - 8, TOK_DEV), f32)
+            rows = bias[i]
+            feat[i] = jnp.transpose(jnp.concatenate([rows, gap, rows, gap], axis=0)).astype(low)
+            return 0
+
+        lax.fori_loop(0, H, one, 0)
+
+    def roots():
+        for number, (ref, t) in enumerate([(root_l, 0), (root_l, 1), (root_r, 0), (root_r, 1)]):
+            load = local(ref.at[t], stg, ks.at[0])
+            load.wait()
+            if number:
+                out.wait()
+
+            def one(i, _):
+                at = pl.ds(pl.multiple_of(i * 96, 96), 96)
+                part = stg[at, :].astype(low).reshape(2, HALF, D)
+                rb[lax.div(i, 2), lax.rem(i, 2)] = part
+                return 0
+
+            lax.fori_loop(0, 8, one, 0)
+            out = local(rb, o_root.at[number], ks.at[1])
+        out.wait()
+
+    def attend(start, stop):
+        def pair(i, _):
+            at = cols(i * 128, 128)
+            q2, k2 = qkv[:, at], qkv[:, cols(D + i * 128, 128)]
+            v2 = qkv[:, cols(2 * D + i * 128, 128)]
+            lane = lax.broadcasted_iota(jnp.int32, (TOK_DEV, 128), 1)
+            row = lax.broadcasted_iota(jnp.int32, (TOK_DEV, 128), 0)
+            spot = (lax.rem(lane, BLK) == lax.div(row, BLK)).astype(f32).astype(low)
+            vT = jnp.transpose(v2)
+            parts = []
+            for half in range(2):
+                mine = (lane < HD) if half == 0 else (lane >= HD)
+                qm = jnp.where(mine, q2, spot)
+                km = jnp.where(mine, k2, feat[2 * i + half])
+                s = lax.dot_general(km, qm, (((1,), (1,)), ((), ())), preferred_element_type=f32)
+                e = jnp.exp(s - jnp.max(s, axis=0, keepdims=True))
+                p = (e * (use_row[...] / jnp.sum(e, axis=0, keepdims=True))).astype(low)
+                P[2 * i + half] = p
+                parts.append(jnp.dot(vT[half * HD : (half + 1) * HD], p, preferred_element_type=f32))
+            total = jnp.where(use_row[...] > 0, jnp.concatenate(parts, axis=0), vT.astype(f32)).astype(low)
+            mT[cols(i * 128, 128), :] = total
+            mix[:, at] = jnp.transpose(total)
+            return 0
+
+        lax.fori_loop(start, stop, pair, 0)
+
+    def flip(source, target):
+        def one(i, _):
+            at = cols(i * 128, 128)
+            target[at, :] = jnp.transpose(source(at))
+            return 0
+
+        lax.fori_loop(0, 6, one, 0)
+
+    def join():
+        def one(i, _):
+            at = cols(i * 256, 256)
+            acc = jnp.dot(mix[...], square(w0, cols(3 * D + i * 256, 256)), preferred_element_type=f32)
+            x1[:, at] = tok_in[:, :, at].reshape(TOK_DEV, 256).astype(f32) + (acc + vt[2:3, at])
+            return 0
+
+        lax.fori_loop(0, 3, one, 0)
+
+    def norm(ref, i):
+        at = pl.ds(pl.multiple_of(i * 64, 64), 64)
+        h = ref[at, :]
+        center = h - jnp.mean(h, axis=1, keepdims=True)
+        r = lax.rsqrt(jnp.mean(center * center, axis=1, keepdims=True) + NORM_EPS)
+        return at, center * r, r
+
+    def norm_one():
+        def one(i, _):
+            at, n, r = norm(x1, i)
+            n1[at, :] = n
+            r1[at, :] = jnp.broadcast_to(r, (64, 128))
+            out = n * vt[4:5, :] + vt[5:6, :]
+            u[at, :] = out.astype(low)
+            x1[at, :] = out
+            return 0
+
+        lax.fori_loop(0, 8, one, 0)
+
+    def lift():
+        for row in range(4):
+
+            def one(i, _, row=row):
+                at = cols(i * 256, 256)
+                to = cols(row * D + i * 256, 256)
+                pre = jnp.dot(u[...], square(w1, to), preferred_element_type=f32) + vt[8 + row : 9 + row, at]
+                sq = pre * pre
+                t = jnp.tanh(0.7978845608028654 * pre * (1.0 + 0.044715 * sq))
+                half = 0.5 * (1.0 + t)
+                fa[:, to] = (pre * half).astype(low)
+                slope = 0.7978845608028654 * (1.0 + 0.134145 * sq)
+                dg[:, to] = (half + 0.5 * pre * (1.0 - t * t) * slope).astype(low)
+                return 0
+
+            lax.fori_loop(0, 3, one, 0)
+
+    def drop():
+        def one(i, _):
+            at = cols(i * 512, 512)
+            acc = lax.dot_general(
+                fa[:, at], square(w2, at), (((1,), (1,)), ((), ())), preferred_element_type=f32
+            )
+            x1[...] += acc
+            return 0
+
+        lax.fori_loop(0, 6, one, 0)
+
+    def norm_two():
+        def one(i, _):
+            at = pl.ds(pl.multiple_of(i * 64, 64), 64)
+            x1[at, :] = x1[at, :] + vt[3:4, :]
+            at, n, r = norm(x1, i)
+            n2[at, :] = n
+            r2[at, :] = jnp.broadcast_to(r, (64, 128))
+            out = (n * vt[6:7, :] + vt[7:8, :]) * use[at, 0:1]
+            yo[at, :] = out.astype(low)
+            return 0
+
+        lax.fori_loop(0, 8, one, 0)
+
+    stays = [narrow(0)]
+    order(tok, tok_s)
+    wait_all()
+    z0 = z_send(0)
+    small = rows_out(vec, vec_in, 2)
+    own = [local(vec, vec_in.at[f], ls.at[5]), local(tok_s.at[f], tok_in.at[f], ls.at[3])]
+    t0 = rows_out(tok_s, tok_in, 0)
+    stays.append(narrow(1))
+    z1 = z_send(1)
+    stays.append(narrow(2))
+    order(cot, cot_s)
+    own.append(local(cot_s.at[f], cot_in.at[f], ls.at[4]))
+    for copy in stays + own:
+        copy.wait()
+    features()
+    p0 = plane(0, z0)
+    for copy in small:
+        copy.wait_recv()
+    wide_vec = jnp.transpose(vec_in[...].reshape(D, 128).astype(f32))
+    vt[...] = wide_vec[:16, :]
+    keep(vt, o_vt)
+    roots()
+    d0 = turn(0, p0)
+    z2 = z_send(2)
+    t1 = rows_out(cot_s, cot_in, 1)
+    last(0, d0)
+    for copy in t0:
+        copy.wait_recv()
+    ready(0)
+    project()
+    keep(qkv, o_qkv)
+    flip(lambda at: tok_in[:, :, at].reshape(TOK_DEV, 128), xT)
+    keep(xT, o_x)
+    p1 = plane(1, z1)
+    attend(0, 2)
+    d1 = turn(1, p1)
+    attend(2, 4)
+    last(1, d1)
+    p2 = plane(2, z2)
+    attend(4, 6)
+    keep(P, o_p)
+    keep(mT, o_mix)
+    join()
+    norm_one()
+    keep(n1, o_n1)
+    keep(r1, o_r1)
+    d2 = turn(2, p2)
+    flip(lambda at: u[:, at], uT)
+    keep(uT, o_u)
+    ready(1)
+    lift()
+    keep(fa, o_f)
+    keep(dg, o_dg)
+    last(2, d2)
+    ready(2)
+    drop()
+    norm_two()
+    keep(n2, o_n2)
+    keep(r2, o_r2)
+    keep(yo, o_y)
+    for copy in t1:
+        copy.wait_recv()
+    keep(cot_in, o_cot)
+    for copy in sent:
+        copy.wait_send()
+    for copy in outs:
+        copy.wait()
+
+
+def forward_all(outrow, tok, cot, flat_weights, vec, bias, use, use_row, root_l, root_r):
+    any_spec = pl.BlockSpec(memory_space=pl.ANY)
+    vmem = pl.BlockSpec(memory_space=pltpu.VMEM)
+    dma = pltpu.SemaphoreType.DMA
+    shape = jax.ShapeDtypeStruct
+    low, f32 = jnp.bfloat16, jnp.float32
+    square = (4, 2, 2, HALF, GCOLS)
+    saved = [
+        ((16, D), f32), ((D, TOK_DEV), low), ((8, 64, D), low), ((TOK_DEV, 3 * D), low),
+        ((H, TOK_DEV, TOK_DEV), low), ((D, TOK_DEV), low), ((TOK_DEV, D), f32), ((TOK_DEV, 128), f32),
+        ((D, TOK_DEV), low), ((TOK_DEV, FF), low), ((TOK_DEV, FF), low), ((TOK_DEV, D), f32),
+        ((TOK_DEV, 128), f32), ((TOK_DEV, D), low), ((4, 4, 2, 2, HALF, D), low),
+    ]
+    return pl.pallas_call(
+        forward_kernel,
+        out_shape=[shape(square, low)] * 3 + [shape(*s) for s in saved],
+        in_specs=[vmem] * 8 + [any_spec] * 2,
+        out_specs=[any_spec] * 18,
+        scratch_shapes=[
+            pltpu.VMEM(square, low), pltpu.VMEM(square, low), pltpu.VMEM(square, low),
+            pltpu.VMEM((8, 64, D), low), pltpu.VMEM((8, 64, D), low), pltpu.VMEM((8, 96, 128), low),
+            pltpu.VMEM((8, 64, D), low), pltpu.VMEM((8, 64, D), low),
+            pltpu.VMEM((16, D), f32),
+            pltpu.VMEM((TOK_DEV, 3 * D), low),
+            pltpu.VMEM((H, TOK_DEV, TOK_DEV), low),
+            pltpu.VMEM((TOK_DEV, D), low),
+            pltpu.VMEM((TOK_DEV, D), f32),
+            pltpu.VMEM((TOK_DEV, 128), f32),
+            pltpu.VMEM((TOK_DEV, D), f32),
+            pltpu.VMEM((TOK_DEV, D), low),
+            pltpu.VMEM((TOK_DEV, FF), low),
+            pltpu.VMEM((TOK_DEV, FF), low),
+            pltpu.VMEM((TOK_DEV, D), f32),
+            pltpu.VMEM((TOK_DEV, 128), f32),
+            pltpu.VMEM((TOK_DEV, D), low),
+            pltpu.VMEM((D, TOK_DEV), low), pltpu.VMEM((D, TOK_DEV), low), pltpu.VMEM((D, TOK_DEV), low),
+            pltpu.VMEM((H, TOK_DEV, 128), low),
+            pltpu.VMEM((D, D), f32),
+            pltpu.VMEM((4, 2, 2, HALF, D), low),
+            pltpu.VMEM((2, HALF, 3 * GCOLS), low),
+            dma((3, 3)), dma((3, 3)), dma((3, 3)), dma((3, 3)), dma((3, 3)), dma((3, 3)),
+            dma((3, 2, 3)), dma((3, 2, 3)), dma((3, 4)), dma((3, 4)),
+            dma((6,)), dma((3, 7)), dma((3, 7)), dma((17,)), dma((2,)),
+        ],
+        compiler_params=pltpu.CompilerParams(
+            collective_id=0, has_side_effects=True, vmem_limit_bytes=60 * MIB
+        ),
+        name="forward_all",
+    )(outrow, tok, cot, flat_weights.reshape(2, HALF, 3 * GCOLS), vec, bias, use, use_row, root_l, root_r)
+
+
+def backward_kernel(
+    block_of, vt, use, use_row,
+    h_w0, h_w1, h_w2, h_xT, h_cot, h_qkv, h_p, h_mT, h_n1, h_r1, h_uT, h_f, h_dg, h_n2, h_r2, h_y, h_root,
+    o_back, o_grad, WR, UA, SC, o_gs, o_vec,
+    G, Rc, A1, A2, B1, B2, ZR, F, SO, Gs, wa, wb, fb, gb, low_g, LT, LU, hb, nb, PT, r1, r2, gi,
+    PQ, sq, sr_in, sc_out, vb, vr,
+    ld, pd, cs, cr, a1s, a1r, b1s, b1r, a2s, a2r, b2s, b2r, zs, zr,
+    fs, fr, ts, tr, ss, sr, ps, pr, us, ur, qs, qr, es, er, ms, mr, vs, vrs, ls,
+):
+    low, f32 = jnp.bfloat16, jnp.float32
+    here = Here(True)
+    wait_all = here.greet()
+    x, y, z, c, f, r = here.x, here.y, here.z, here.c, here.f, here.r
+    W = GCOLS // 2
+    sent = []
+
+    class Load:
+        def __init__(self, number, src, dst):
+            self.copy, self.done = local(src, dst, ld.at[number]), False
+
+        def wait(self):
+            if not self.done:
+                self.copy.wait()
+                self.done = True
+
+    cot_l = Load(0, h_cot, gi)
+    n2_l = Load(1, h_n2, hb)
+    r2_l = Load(2, h_r2, r2)
+    f_l = Load(3, h_f, fb)
+    wd_l = Load(4, h_w2, wa)
+    dg_l = Load(5, h_dg, gb)
+    uT_l = Load(6, h_uT, LU)
+    wu_l = Load(7, h_w1, wb)
+    n1_l = Load(8, h_n1, nb)
+    r1_l = Load(9, h_r1, r1)
+    vb[...] = jnp.zeros_like(vb)
+    wait_all()
+
+    def span(g):
+        return pl.ds(g * W, W)
+
+    def c_send(g):
+        copy = send(
+            G.at[:, :, 1 - c, :, :, span(g)], Rc.at[:, :, :, :, span(g)],
+            cs.at[g], cr.at[g], here.to_core,
+        )
+        sent.append(copy)
+        return copy
+
+    def first(g, copy):
+        copy.wait_recv()
+
+        def add(i, _):
+            j, zz, h = lax.div(i, 8), lax.rem(lax.div(i, 2), 4), lax.rem(i, 2)
+            G[j, zz, c, h, :, span(g)] = (
+                G[j, zz, c, h, :, span(g)].astype(f32) + Rc[j, zz, h, :, span(g)].astype(f32)
+            ).astype(low)
+            return 0
+
+        lax.fori_loop(0, 16, add, 0)
+        a = send(
+            G.at[:, 0:2, c, 1 - x, :, span(g)], A1.at[:, :, :, span(g)], a1s.at[g], a1r.at[g], here.to_x
+        )
+        b = send(
+            G.at[1 - y, 2:4, c, :, :, span(g)], B1.at[:, :, :, span(g)], b1s.at[g], b1r.at[g], here.to_y
+        )
+        sent.extend([a, b])
+        return a, b
+
+    def second(g, copies):
+        copies[0].wait_recv()
+
+        def add_a(i, _):
+            j, zz = lax.div(i, 2), lax.rem(i, 2)
+            G[j, zz, c, x, :, span(g)] = (
+                G[j, zz, c, x, :, span(g)].astype(f32) + A1[j, zz, :, span(g)].astype(f32)
+            ).astype(low)
+            return 0
+
+        lax.fori_loop(0, 4, add_a, 0)
+        a = send(
+            G.at[1 - y, 0:2, c, x, :, span(g)], A2.at[:, :, span(g)], a2s.at[g], a2r.at[g], here.to_y
+        )
+        copies[1].wait_recv()
+
+        def add_b(i, _):
+            zz, h = lax.div(i, 2), lax.rem(i, 2)
+            G[y, zz + 2, c, h, :, span(g)] = (
+                G[y, zz + 2, c, h, :, span(g)].astype(f32) + B1[zz, h, :, span(g)].astype(f32)
+            ).astype(low)
+            return 0
+
+        lax.fori_loop(0, 4, add_b, 0)
+        b = send(
+            G.at[y, 2:4, c, 1 - x, :, span(g)], B2.at[:, :, span(g)], b2s.at[g], b2r.at[g], here.to_x
+        )
+        sent.extend([a, b])
+        return a, b
+
+    def third(g, copies):
+        for number, (copy, part) in enumerate(zip(copies, (A2, B2))):
+            copy.wait_recv()
+
+            def add(i, _, number=number, part=part):
+                zz = 2 * number + i
+                G[y, zz, c, x, :, span(g)] = (
+                    G[y, zz, c, x, :, span(g)].astype(f32) + part[i, :, span(g)].astype(f32)
+                ).astype(low)
+                return 0
+
+            lax.fori_loop(0, 2, add, 0)
+        out = []
+        for step in (1, 2, 3):
+            out.append(
+                send(
+                    G.at[y, here.z_plus(step), c, x, :, span(g)], ZR.at[step - 1, :, span(g)],
+                    zs.at[g, step - 1], zr.at[g, step - 1], here.along(step),
+                )
+            )
+        sent.extend(out)
+        return out
+
+    def final(g, copies):
+        for copy in copies:
+            copy.wait_recv()
+        for b in range(4 * g, 4 * g + 4):
+            at = pl.ds(b * JCOLS, JCOLS)
+            total = G[y, z, c, x, :, at].astype(f32)
+            for step in range(3):
+                total = total + ZR[step, :, at].astype(f32)
+            F[b] = total.astype(low)
+
+    homes = []
+
+    def spread(g):
+        at = pl.ds(4 * g, 4)
+        to = WR.at[x, y, at]
+        a = send(F.at[at], to, fs.at[g, 0], fr.at[g, 0], here.to_x)
+        b = send(F.at[at], to, fs.at[g, 1], fr.at[g, 1], here.to_y)
+        homes.append(local(F.at[at], to, ls.at[g]))
+        sent.extend([a, b])
+        return a, b
+
+    def spread_on(g, copies):
+        a, b = copies
+        a.wait_recv()
+        part = WR.at[1 - x, y, pl.ds(4 * g, 2)]
+        da = send(part, part, fs.at[g, 2], fr.at[g, 2], here.to_y)
+        b.wait_recv()
+        part = WR.at[x, 1 - y, pl.ds(4 * g + 2, 2)]
+        db = send(part, part, fs.at[g, 3], fr.at[g, 3], here.to_x)
+        sent.extend([da, db])
+        return da, db
+
+    def token_send(source, landing, number):
+        out = []
+        for step in range(1, 8):
+            to = here.peer(step)
+            out.append(
+                send(source(to), landing.at[f], ts.at[number, step - 1], tr.at[number, step - 1], (r, to))
+            )
+        homes.append(local(source(f), landing.at[f], ls.at[3 + number]))
+        sent.extend(out)
+        return out
+
+    def square(ref, at):
+        return ref[:, :, :, :, at].reshape(D, at.size)
+
+    def own_rows(ref, core):
+        return jnp.concatenate(
+            [ref[pl.ds(pl.multiple_of((2 * zz + core) * 96, 96), 96), :] for zz in range(4)], axis=0
+        )
+
+    def gradient(left, right, block, start, count, core):
+        rows = own_rows(left, core)
+
+        def one(i, _):
+            out = jnp.dot(rows, right[:, cols(start + i * D, D)], preferred_element_type=f32)
+            out = out.astype(low).reshape(4, 2, HALF, D)
+            for j in range(2):
+                at = cols((block + i) * JCOLS, JCOLS)
+                G[j, :, core, :, :, at] = out[:, :, :, j * JCOLS : (j + 1) * JCOLS]
+            return 0
+
+        lax.fori_loop(0, count, one, 0)
+
+    def eight(v):
+        return jnp.sum(v.reshape(8, 8, v.shape[1]), axis=0)
+
+    def norm_back(i, carry, grad, n, rr, gain):
+        zed = grad * gain
+        back = rr * (
+            zed - jnp.mean(zed, axis=1, keepdims=True) - n * jnp.mean(zed * n, axis=1, keepdims=True)
+        )
+        rounded = back.astype(low)
+        return back, rounded, (
+            carry[0] + eight(grad * n), carry[1] + eight(grad), carry[2] + eight(rounded.astype(f32))
+        )
+
+    zero = jnp.zeros((8, D), f32)
+
+    def put(row, total):
+        vb[0, row : row + 1, :] = jnp.sum(total, axis=0, keepdims=True)
+
+    def flip(source, target, count):
+        def one(i, _):
+            at = cols(i * 128, 128)
+            target[at, :] = jnp.transpose(source[:, at])
+            return 0
+
+        lax.fori_loop(0, count, one, 0)
+
+    ta = token_send(lambda to: h_y.at[to], o_back, 0)
+    cot_l.wait()
+    n2_l.wait()
+    r2_l.wait()
+
+    def back_two(i, carry):
+        at = pl.ds(pl.multiple_of(i * 64, 64), 64)
+        grad = gi[i].astype(f32) * use[at, 0:1]
+        back, rounded, carry = norm_back(i, carry, grad, hb[at, :], r2[at, 0:1], vt[6:7, :])
+        hb[at, :] = back
+        low_g[at, :] = rounded
+        return carry
+
+    sums = lax.fori_loop(0, 8, back_two, (zero, zero, zero))
+    put(6, sums[0])
+    put(7, sums[1])
+    put(3, sums[2])
+    flip(low_g, LT, 6)
+    f_l.wait()
+    gradient(LT, fb, 8, 0, 4, 1 - c)
+    c2 = c_send(2)
+    gradient(LT, fb, 8, 0, 4, c)
+    qkv_l = Load(10, h_qkv, fb.at[:, : 3 * D])
+    mT_l = Load(11, h_mT, LT)
+    wd_l.wait()
+    dg_l.wait()
+
+    def back_up(i, _):
+        at = cols(i * 256, 256)
+        acc = jnp.dot(low_g[...], square(wa, at), preferred_element_type=f32)
+        gb[:, at] = (acc * gb[:, at].astype(f32)).astype(low)
+        return 0
+
+    lax.fori_loop(0, 12, back_up, 0)
+    wq_l = Load(12, h_w0, wa)
+    f2 = first(2, c2)
+    uT_l.wait()
+    gradient(LU, gb, 4, 0, 4, 1 - c)
+    c1 = c_send(1)
+    gradient(LU, gb, 4, 0, 4, c)
+    xT_l = Load(13, h_xT, LU)
+    wu_l.wait()
+
+    def back_x1(i, _):
+        at = cols(i * 512, 512)
+        hb[...] += lax.dot_general(
+            gb[:, at], square(wb, at), (((1,), (1,)), ((), ())), preferred_element_type=f32
+        )
+        return 0
+
+    lax.fori_loop(0, 6, back_x1, 0)
+    root_l = [Load(14 + n, h_root.at[n], wb.at[:, :, :, :, n * D : (n + 1) * D]) for n in range(4)]
+    for row in range(4):
+
+        def total(i, acc, row=row):
+            at = pl.ds(pl.multiple_of(i * 64, 64), 64)
+            return acc + eight(gb[at, row * D : (row + 1) * D].astype(f32))
+
+        put(8 + row, lax.fori_loop(0, 8, total, zero))
+    f1 = first(1, c1)
+    n1_l.wait()
+    r1_l.wait()
+
+    def back_one(i, carry):
+        at = pl.ds(pl.multiple_of(i * 64, 64), 64)
+        back, rounded, carry = norm_back(i, carry, hb[at, :], nb[at, :], r1[at, 0:1], vt[4:5, :])
+        hb[at, :] = back
+        low_g[at, :] = rounded
+        return carry
+
+    sums = lax.fori_loop(0, 8, back_one, (zero, zero, zero))
+    put(4, sums[0])
+    put(5, sums[1])
+    put(2, sums[2])
+    s2 = second(2, f2)
+    mT_l.wait()
+    gradient(LT, low_g, 3, 0, 1, 1 - c)
+    gradient(LT, low_g, 3, 0, 1, c)
+    wq_l.wait()
+
+    def back_mix(i, _):
+        out = lax.dot_general(
+            low_g[...], wa[pl.ds(2 * i, 2), :, :, :, 3 * D : 4 * D].reshape(JCOLS, D),
+            (((1,), (1,)), ((), ())), preferred_element_type=f32,
+        )
+        gb[:, cols(3 * D + i * JCOLS, JCOLS)] = out.astype(low)
+        return 0
+
+    lax.fori_loop(0, 2, back_mix, 0)
+    qkv_l.wait()
+
+    def fetch(i):
+        return pltpu.make_async_copy(h_p.at[pl.ds(2 * i, 2)], PT.at[lax.rem(i, 2)], pd.at[lax.rem(i, 2)])
+
+    fetch(0).start()
+
+    def attend(i, _):
+        slot = lax.rem(i, 2)
+
+        @pl.when(i < 5)
+        def _():
+            fetch(i + 1).start()
+
+        q2, k2 = fb[:, cols(i * 128, 128)], fb[:, cols(D + i * 128, 128)]
+        v2, go2 = fb[:, cols(2 * D + i * 128, 128)], gb[:, cols(3 * D + i * 128, 128)]
+        kT = jnp.transpose(k2)
+        lane = lax.broadcasted_iota(jnp.int32, (TOK_DEV, 128), 1)
+        fetch(i).wait()
+        parts = []
+        gk = jnp.zeros((TOK_DEV, 128), f32)
+        gv = jnp.where(use[:, :] > 0, 0.0, go2.astype(f32))
+        for half in range(2):
+            mine = (lane < HD) if half == 0 else (lane >= HD)
+            none = jnp.zeros_like(v2)
+            p = PT[slot, half]
+            gp = lax.dot_general(
+                jnp.where(mine, v2, none), go2, (((1,), (1,)), ((), ())), preferred_element_type=f32
+            )
+            pf = p.astype(f32)
+            gs = (pf * (gp - jnp.sum(pf * gp, axis=0, keepdims=True))).astype(low)
+            gk = gk + jnp.dot(gs, jnp.where(mine, q2, none), preferred_element_type=f32)
+            gv = gv + jnp.dot(p, jnp.where(mine, go2, none), preferred_element_type=f32)
+            parts.append(jnp.dot(kT[half * HD : (half + 1) * HD], gs, preferred_element_type=f32))
+        gq = jnp.transpose(jnp.concatenate(parts, axis=0)) * (HD ** (-0.5))
+        gb[:, cols(i * 128, 128)] = gq.astype(low)
+        gb[:, cols(D + i * 128, 128)] = gk.astype(low)
+        gb[:, cols(2 * D + i * 128, 128)] = gv.astype(low)
+        return 0
+
+    lax.fori_loop(0, 2, attend, 0)
+    s1 = second(1, f1)
+    t2 = third(2, s2)
+    lax.fori_loop(2, 4, attend, 0)
+    t1 = third(1, s1)
+    lax.fori_loop(4, 6, attend, 0)
+    xT_l.wait()
+    gradient(LU, gb, 0, 0, 3, 1 - c)
+    c0 = c_send(0)
+    gradient(LU, gb, 0, 0, 3, c)
+    for row, start in ((0, 0), (1, 2 * D)):
+
+        def total(i, acc, start=start):
+            at = pl.ds(pl.multiple_of(i * 64, 64), 64)
+            return acc + eight(gb[at, start : start + D].astype(f32))
+
+        put(row, lax.fori_loop(0, 8, total, zero))
+    f0 = first(0, c0)
+    vec_copy = send(vb.at[0], vr.at[0], vs.at[0], vrs.at[0], here.to_core)
+    sent.append(vec_copy)
+    final(2, t2)
+    e2 = spread(2)
+
+    def back_x(i, _):
+        at = cols(i * D, D)
+        hb[...] += lax.dot_general(
+            gb[:, at], square(wa, at), (((1,), (1,)), ((), ())), preferred_element_type=f32
+        )
+        return 0
+
+    lax.fori_loop(0, 3, back_x, 0)
+
+    def rows_low(i, _):
+        gi[i] = hb[pl.ds(pl.multiple_of(i * 64, 64), 64), :].astype(low)
+        return 0
+
+    lax.fori_loop(0, 8, rows_low, 0)
+    vec_copy.wait_recv()
+    vb[1] = vb[0] + vr[0]
+    vec_copy = send(vb.at[1], vr.at[1], vs.at[1], vrs.at[1], here.to_x)
+    sent.append(vec_copy)
+    s0 = second(0, f0)
+    final(1, t1)
+    e1 = spread(1)
+    vec_copy.wait_recv()
+    vb[2] = vb[1] + vr[1]
+    vec_copy = send(vb.at[2], vr.at[2], vs.at[2], vrs.at[2], here.to_y)
+    sent.append(vec_copy)
+    d2 = spread_on(2, e2)
+    t0 = third(0, s0)
+    final(0, t0)
+    jc = cols(y * JCOLS, JCOLS)
+    other = cols((1 - y) * JCOLS, JCOLS)
+    slot_copies = []
+    for step in range(1, 9):
+        to = here.peer(step)
+        for t in range(2):
+            b = block_of[2 * to + t]
+            flag = (b >= 0).astype(f32)
+            SO[step - 1, t] = (F[jnp.maximum(b, 0)].astype(f32) * flag).astype(low)
+        if step < 8:
+            slot_copies.append(
+                send(SO.at[step - 1], Gs.at[:, f, x, :, jc], ss.at[step - 1], sr.at[step - 1], (r, to))
+            )
+    sent.extend(slot_copies)
+    own = local(SO.at[7], Gs.at[:, f, x, :, jc], ls.at[5])
+    hops = []
+    for step in range(8):
+        src = lax.rem(f + 8 - step, 8)
+        if step == 0:
+            own.wait()
+        else:
+            slot_copies[step - 1].wait_recv()
+        part = Gs.at[:, src, x, :, jc]
+        hops.append(
+            (
+                send(part, part, ps.at[0, step], pr.at[0, step], here.to_x),
+                send(part, part, ps.at[1, step], pr.at[1, step], here.to_y),
+            )
+        )
+    ends = []
+    for step in range(8):
+        src = lax.rem(f + 8 - step, 8)
+        hops[step][0].wait_recv()
+        part = Gs.at[0, src, 1 - x, :, jc]
+        ends.append(send(part, part, ps.at[2, step], pr.at[2, step], here.to_y))
+        hops[step][1].wait_recv()
+        part = Gs.at[1, src, x, :, other]
+        ends.append(send(part, part, ps.at[3, step], pr.at[3, step], here.to_x))
+        sent.extend(hops[step])
+    sent.extend(ends)
+    vec_copy.wait_recv()
+    vb[3] = vb[2] + vr[2]
+    vec_copies = []
+    for step in (1, 2, 3):
+        vec_copies.append(
+            send(vb.at[3], vr.at[2 + step], vs.at[2 + step], vrs.at[2 + step], here.along(step))
+        )
+    sent.extend(vec_copies)
+    e0 = spread(0)
+    d1 = spread_on(1, e1)
+    for load in root_l:
+        load.wait()
+    for copy in ends:
+        copy.wait_recv()
+    homes.append(local(Gs, o_gs, ls.at[6]))
+    for t in range(2):
+        whole = Gs[t].reshape(D, D)
+        rows = wb[:, :, x, :, t * D : (t + 1) * D].reshape(JCOLS, D)
+        half = jnp.dot(rows, whole, preferred_element_type=f32).astype(low)
+        right = square(wb, cols((2 + t) * D + y * JCOLS, JCOLS))
+        part = jnp.dot(half, right, preferred_element_type=f32)
+        PQ[t] = part.astype(low).reshape(8, HALF, JCOLS)
+        sq[t] = jnp.sum((part * part).reshape(48, 8, JCOLS), axis=0)
+    ucopies = []
+    for step in range(1, 8):
+        to = here.peer(step)
+        ucopies.append(
+            send(PQ.at[:, to], UA.at[x, y, pl.ds(2 * f, 2)], us.at[step - 1], ur.at[step - 1], (r, to))
+        )
+    sent.extend(ucopies)
+    own = local(PQ.at[:, f], UA.at[x, y, pl.ds(2 * f, 2)], ls.at[7])
+    squares = []
+    for number, to in enumerate((here.to_x, here.to_y, here.to_d)):
+        squares.append(send(sq, sr_in.at[number], es.at[number], er.at[number], to))
+    sent.extend(squares)
+    uhops = []
+    for step in range(8):
+        src = lax.rem(f + 8 - step, 8)
+        if step == 0:
+            own.wait()
+        else:
+            ucopies[step - 1].wait_recv()
+        part = UA.at[x, y, pl.ds(2 * src, 2)]
+        uhops.append(
+            (
+                send(part, part, qs.at[0, step], qr.at[0, step], here.to_x),
+                send(part, part, qs.at[1, step], qr.at[1, step], here.to_y),
+            )
+        )
+        if step == 0:
+            for copy in squares:
+                copy.wait_recv()
+            for t in range(2):
+                total = sq[t] + sr_in[0, t] + sr_in[1, t] + sr_in[2, t]
+                mean = jnp.sum(jnp.sum(total, axis=1, keepdims=True), axis=0, keepdims=True) * (1.0 / (D * D))
+                sc_out[t] = jnp.broadcast_to(lax.rsqrt(mean + RMS_EPS), (8, 128))
+            scales = []
+            for number in range(1, 8):
+                to = here.peer(number)
+                scales.append(
+                    send(
+                        sc_out, SC.at[pl.ds(2 * f, 2)], ms.at[number - 1], mr.at[number - 1], (r, to)
+                    )
+                )
+            sent.extend(scales)
+            homes.append(local(sc_out, SC.at[pl.ds(2 * f, 2)], ls.at[8]))
+            tb = token_send(lambda to: gi.at[to], o_grad, 1)
+    uends = []
+    for step in range(8):
+        src = lax.rem(f + 8 - step, 8)
+        uhops[step][0].wait_recv()
+        part = UA.at[1 - x, y, 2 * src]
+        uends.append(send(part, part, qs.at[2, step], qr.at[2, step], here.to_y))
+        uhops[step][1].wait_recv()
+        part = UA.at[x, 1 - y, 2 * src + 1]
+        uends.append(send(part, part, qs.at[3, step], qr.at[3, step], here.to_x))
+        sent.extend(uhops[step])
+    sent.extend(uends)
+    d0 = spread_on(0, e0)
+    total = vb[3]
+    for copy in vec_copies:
+        copy.wait_recv()
+    for step in range(3):
+        total = total + vr[3 + step]
+    vb[4] = total
+    homes.append(local(vb.at[4], o_vec, ls.at[9]))
+    for copy in list(d2) + list(d1) + list(d0) + uends + scales + ta + tb:
+        copy.wait_recv()
+    for copy in homes:
+        copy.wait()
+    for copy in sent:
+        copy.wait_send()
+
+
+def backward_all(block_of, vt, use, use_row, saved):
+    any_spec = pl.BlockSpec(memory_space=pl.ANY)
+    vmem = pl.BlockSpec(memory_space=pltpu.VMEM)
+    smem = pl.BlockSpec(memory_space=pltpu.SMEM)
+    dma = pltpu.SemaphoreType.DMA
+    shape = jax.ShapeDtypeStruct
+    low, f32 = jnp.bfloat16, jnp.float32
+    JW = 12 * JCOLS
+    square = (4, 2, 2, HALF, GCOLS)
+    return pl.pallas_call(
+        backward_kernel,
+        out_shape=[
+            shape((8, 64, D), low), shape((8, 64, D), low),
+            shape((2, 2, 12, HALF, JCOLS), low), shape((2, 2, 16, HALF, JCOLS), low),
+            shape((16, 8, 128), f32), shape((2, 8, 2, HALF, D), low), shape((16, D), f32),
+        ],
+        in_specs=[smem, vmem, vmem, vmem] + [any_spec] * 17,
+        out_specs=[any_spec] * 7,
+        scratch_shapes=[
+            pltpu.VMEM((2, 4, 2, 2, HALF, JW), low),
+            pltpu.VMEM((2, 4, 2, HALF, JW), low),
+            pltpu.VMEM((2, 2, HALF, JW), low),
+            pltpu.VMEM((2, HALF, JW), low),
+            pltpu.VMEM((2, 2, HALF, JW), low),
+            pltpu.VMEM((2, HALF, JW), low),
+            pltpu.VMEM((3, HALF, JW), low),
+            pltpu.VMEM((12, HALF, JCOLS), low),
+            pltpu.VMEM((8, 2, HALF, JCOLS), low),
+            pltpu.VMEM((2, 8, 2, HALF, D), low),
+            pltpu.VMEM(square, low),
+            pltpu.VMEM(square, low),
+            pltpu.VMEM((TOK_DEV, FF), low),
+            pltpu.VMEM((TOK_DEV, FF), low),
+            pltpu.VMEM((TOK_DEV, D), low),
+            pltpu.VMEM((D, TOK_DEV), low),
+            pltpu.VMEM((D, TOK_DEV), low),
+            pltpu.VMEM((TOK_DEV, D), f32),
+            pltpu.VMEM((TOK_DEV, D), f32),
+            pltpu.VMEM((2, 2, TOK_DEV, TOK_DEV), low),
+            pltpu.VMEM((TOK_DEV, 128), f32),
+            pltpu.VMEM((TOK_DEV, 128), f32),
+            pltpu.VMEM((8, 64, D), low),
+            pltpu.VMEM((2, 8, HALF, JCOLS), low),
+            pltpu.VMEM((2, 8, JCOLS), f32),
+            pltpu.VMEM((3, 2, 8, JCOLS), f32),
+            pltpu.VMEM((2, 8, 128), f32),
+            pltpu.VMEM((5, 16, D), f32),
+            pltpu.VMEM((6, 16, D), f32),
+            dma((18,)), dma((2,)), dma((3,)), dma((3,)),
+            dma((3,)), dma((3,)), dma((3,)), dma((3,)), dma((3,)), dma((3,)), dma((3,)), dma((3,)),
+            dma((3, 3)), dma((3, 3)), dma((3, 4)), dma((3, 4)),
+            dma((2, 7)), dma((2, 7)), dma((7,)), dma((7,)), dma((4, 8)), dma((4, 8)),
+            dma((7,)), dma((7,)), dma((4, 8)), dma((4, 8)), dma((3,)), dma((3,)), dma((7,)), dma((7,)),
+            dma((6,)), dma((6,)), dma((10,)),
+        ],
+        compiler_params=pltpu.CompilerParams(
+            collective_id=1, has_side_effects=True, vmem_limit_bytes=60 * MIB
+        ),
+        name="backward_all",
+    )(block_of, vt, use, use_row, *saved)
+
+
+def finish_kernel(
+    owner, outrow, back, grad, wr, ua, sc, gs, vec, stat_l, stat_r, wf, vecs, mom1, mom2,
+    layer_out, input_grad, wg, nw, new_l, new_r, out1, out2, outv,
+    gb, sl, sr, ub, rb, wb, nb, gg, tb, to, ls, os,
+):
+    low, f32 = jnp.bfloat16, jnp.float32
+    f = lax.axis_index("fsdp")
+    loads = [
+        local(back, tb.at[0], ls.at[0]), local(grad, tb.at[1], ls.at[1]),
+        local(wr, rb, ls.at[2]), local(ua, ub, ls.at[3]), local(wf, wb, ls.at[4]),
+        local(gs, gb, ls.at[5]),
+    ]
+    stats = [
+        (local(stat_l.at[t], sl.at[t], ls.at[6 + 2 * t]), local(stat_r.at[t], sr.at[t], ls.at[7 + 2 * t]))
+        for t in range(2)
+    ]
+    outs = []
+    hot = (outrow[...] == lax.broadcasted_iota(jnp.int32, (TOK_DEV, TOK_DEV), 1)).astype(f32).astype(low)
+    for number, target in enumerate((layer_out, input_grad)):
+        loads[number].wait()
+        to[number] = jnp.dot(
+            hot, tb[number].reshape(TOK_DEV, D), preferred_element_type=f32
+        ).astype(low)
+        outs.append(local(to.at[number], target, os.at[number]))
+    loads[2].wait()
+
+    def one(i, _):
+        h, b = lax.rem(i, 2), lax.div(i, 2)
+        for j in range(2):
+            gg[h, :, cols(b * D + j * JCOLS, JCOLS)] = rb[h, j, b].astype(f32)
+        return 0
+
+    lax.fori_loop(0, 24, one, 0)
+    outs.append(local(gg, wg, os.at[2]))
+    loads[3].wait()
+    loads[4].wait()
+    for b in range(NBLK):
+        slot = owner[b]
+        scale = LR_MATRIX * sc[slot, 0:1, 0:1]
+        for h in range(2):
+            for j in range(2):
+                at = pl.ds(b * D + j * JCOLS, JCOLS)
+                nb[h, :, at] = wb[h, :, at] - scale * ub[h, j, slot].astype(f32)
+    outs.append(local(nb, nw, os.at[3]))
+    loads[5].wait()
+    for t in range(2):
+        stats[t][0].wait()
+
+        def left(i, _, t=t):
+            at = pl.ds(pl.multiple_of(i * 192, 192), 192)
+            rows = gb[t, pl.ds(2 * i, 2)].reshape(192, D)
+            part = lax.dot_general(
+                rows, gb[t].reshape(D, D), (((1,), (1,)), ((), ())), preferred_element_type=f32
+            )
+            sl[t, at, :] = STAT_DECAY * sl[t, at, :] + (1.0 - STAT_DECAY) * part
+            return 0
+
+        lax.fori_loop(0, 4, left, 0)
+        outs.append(local(sl.at[t], new_l.at[t], os.at[4 + 2 * t]))
+        stats[t][1].wait()
+        for i in range(3):
+            at = pl.ds(i * 256, 256)
+            part = lax.dot_general(
+                gb[t, :, :, :, at].reshape(D, 256), gb[t].reshape(D, D), (((0,), (0,)), ((), ())),
+                preferred_element_type=f32,
+            )
+            sr[t, at, :] = STAT_DECAY * sr[t, at, :] + (1.0 - STAT_DECAY) * part
+        outs.append(local(sr.at[t], new_r.at[t], os.at[5 + 2 * t]))
+    tall = jnp.transpose(jnp.concatenate([vec[...], jnp.zeros((112, D), f32)], axis=0))
+    gi = to.at[0]
+    mine = jnp.zeros((96, NBLK), f32)
+    for number in range(8):
+        part = tall[number * 96 : (number + 1) * 96, :NBLK]
+        mine = jnp.where(f == number, part, mine)
+    fresh1 = BETA_ONE * mom1[...] + (1.0 - BETA_ONE) * mine
+    fresh2 = BETA_TWO * mom2[...] + (1.0 - BETA_TWO) * mine * mine
+    out1[...] = fresh1
+    out2[...] = fresh2
+    outv[...] = vecs[...] - LR_VECTOR * (fresh1 / (1.0 - BETA_ONE**STEP)) / (
+        jnp.sqrt(fresh2 / (1.0 - BETA_TWO**STEP)) + ADAM_EPS
+    )
+    for copy in outs:
+        copy.wait()
+
+
+def finish_all(owner, outrow, results, stat_l, stat_r, wf, vecs, mom1, mom2):
+    any_spec = pl.BlockSpec(memory_space=pl.ANY)
+    vmem = pl.BlockSpec(memory_space=pltpu.VMEM)
+    smem = pl.BlockSpec(memory_space=pltpu.SMEM)
+    dma = pltpu.SemaphoreType.DMA
+    shape = jax.ShapeDtypeStruct
+    low, f32 = jnp.bfloat16, jnp.float32
+    wide = (2, HALF, 3 * GCOLS)
+    back, grad, wr, ua, sc, gs, vec = results
+    return pl.pallas_call(
+        finish_kernel,
+        out_shape=[
+            shape((TOK_DEV, D), low), shape((TOK_DEV, D), low), shape(wide, f32), shape(wide, f32),
+            shape((2, D, D), f32), shape((2, D, D), f32),
+            shape((96, NBLK), f32), shape((96, NBLK), f32), shape((96, NBLK), f32),
+        ],
+        in_specs=[smem, vmem] + [any_spec] * 4 + [vmem, any_spec, vmem] + [any_spec] * 3 + [vmem] * 3,
+        out_specs=[any_spec] * 6 + [vmem] * 3,
+        scratch_shapes=[
+            pltpu.VMEM((2, 8, 2, HALF, D), low),
+            pltpu.VMEM((2, D, D), f32),
+            pltpu.VMEM((2, D, D), f32),
+            pltpu.VMEM((2, 2, 16, HALF, JCOLS), low),
+            pltpu.VMEM((2, 2, 12, HALF, JCOLS), low),
+            pltpu.VMEM(wide, f32),
+            pltpu.VMEM(wide, f32),
+            pltpu.VMEM(wide, f32),
+            pltpu.VMEM((2, 8, 64, D), low),
+            pltpu.VMEM((2, TOK_DEV, D), low),
+            dma((10,)), dma((8,)),
+        ],
+        compiler_params=pltpu.CompilerParams(vmem_limit_bytes=56 * MIB),
+        name="finish_all",
+    )(
+        owner, outrow, back, grad, wr, ua, sc, gs, vec, stat_l, stat_r, wf.reshape(wide), vecs, mom1, mom2
+    )
+
+
+def masks(seq_lengths, random_blocks):
+    seq_id, position, in_use, seq_blocks = layout(seq_lengths[0])
+    picks = random_blocks % jnp.maximum(seq_blocks.reshape(TOK_DEV // BLK, BLK)[:, 0], 1)[:, None, None]
+    rows = slice(None, None, BLK)
+    row_seq, row_block = seq_id[rows], position[rows] // BLK
+    key_block = position // BLK
+    same = (row_seq[:, None] == seq_id[None, :]) & in_use[None, :]
+    near = (
+        (row_block[:, None] < NGLOB)
+        | (key_block[None, :] < NGLOB)
+        | (jnp.abs(row_block[:, None] - key_block[None, :]) <= 1)
+    )
+    chosen = jnp.any(picks[:, :, :, None] == key_block[None, None, None, :], axis=2)
+    keep = same[:, None, :] & (near[:, None, :] | chosen)
+    bias = jnp.where(jnp.transpose(keep, (1, 0, 2)), 0.0, MASKED_SCORE).astype(jnp.float32)
+    use = jnp.broadcast_to(in_use.astype(jnp.float32)[:, None], (TOK_DEV, 128))
+    use_row = in_use.astype(jnp.float32)[None, :]
+    return bias, use, use_row
+
+
+def fast_body(
+    tokens,
+    cotangent,
+    place,
+    seq_lengths,
+    random_blocks,
+    owner_slot,
+    flat_weights,
+    vectors,
+    moment_first,
+    moment_second,
+    stat_left,
+    stat_right,
+    root_left,
+    root_right,
+):
+    peers = lax.axis_size("fsdp")
+    share_rows = TOK_DEV // peers
+    me = lax.axis_index("fsdp")
+    outrow = (place // TOK_DEV) * share_rows + place % TOK_DEV - me * share_rows
+    vec_pad = jnp.pad(vectors.astype(jnp.bfloat16), ((0, 0), (0, 128 - NBLK)))
+    bias, use, use_row = masks(seq_lengths, random_blocks)
+    slots = jnp.arange(2 * peers, dtype=jnp.int32)
+    hits = slots[:, None] == owner_slot[None, :]
+    block_of = jnp.sum(jnp.where(hits, jnp.arange(NBLK, dtype=jnp.int32)[None, :] + 1, 0), axis=1) - 1
+    w0, w1, w2, vt, *saved = forward_all(
+        outrow[None, :], tokens, cotangent, flat_weights, vec_pad, bias, use, use_row, root_left, root_right
+    )
+    saved[-2] = saved[-2].reshape(peers, share_rows, D)
+    results = backward_all(block_of.astype(jnp.int32), vt, use, use_row, [w0, w1, w2] + saved)
+    layer_out, input_grad, weight_grads, new_weights, *others = finish_all(
+        owner_slot, outrow[:, None], results, stat_left, stat_right, flat_weights, vectors, moment_first,
+        moment_second,
+    )
+    return (
+        layer_out,
+        input_grad,
+        weight_grads.reshape(flat_weights.shape),
+        new_weights.reshape(flat_weights.shape),
+        *others,
+    )
+
+
+def plain_body(
     tokens,
     cotangent,
     place,
@@ -388,4 +1603,6 @@
         P("fsdp", None),
         P("fsdp", None),
     )
+    shaped = mesh.shape["fsdp"] == 8 and mesh.shape["rep"] == 4
+    body = fast_body if shaped else plain_body
     return jax.shard_map(body, mesh=mesh, in_specs=in_specs, out_specs=out_specs, check_vma=False)

time: 874 us -> 322 us (0.37)
  waiting for transfers between devices: 473 us -> 0 us
  Pallas kernels: 0 us -> 304 us
  matrix products: 129 us -> 0 us
  blocking collectives: 125 us -> 0 us
  other arithmetic: 54.6 us -> 7.58 us
  starting transfers between devices: 33.3 us -> 0 us
  local copies, waits for them, and re-layouts: 38.3 us -> 9.38 us
  between operations: 15.1 us -> 0.74 us
    reduce_scatter x2 -> x0, waiting for transfers between devices: 311 us -> none  [the longest x1 279 us: body(): lax.psum_scatter(jnp.concatenate([attn_mats, ffn_mats], axis=1), 'fsdp',...]
    pallas_call x0 -> x3, Pallas kernels: none -> 304 us  [the longest x1 176 us: backward_all(): pl.pallas_call(backward_kernel, out_shape=[shape((8, 64, D), low), shape(...]
    dot_general x24 -> x0, matrix products: 129 us -> none  [the longest x4 24.1 us: contract_cols(): lax.dot_general(left, right, (((1,), (1,)), ((), ())), preferred_element_...]
    all_gather x2 -> x0, waiting for transfers between devices: 121 us -> none  [the longest x1 86.7 us: body(): lax.all_gather(flat_weights.astype(jnp.bfloat16), 'fsdp', axis=0, tiled=T...]
    all_to_all x1 -> x0, blocking collectives: 57 us -> none  [body(): lax.all_to_all(outbound.astype(jnp.bfloat16), 'fsdp', split_axis=1, conca...]
    all_gather x1 -> x0, blocking collectives: 47.1 us -> none  [body(): lax.all_gather(vectors.astype(jnp.bfloat16), 'fsdp', axis=0, tiled=True)]
    all_to_all x5 -> x0, starting transfers between devices: 32.9 us -> none  [the longest x1 8.04 us: body(): lax.all_to_all(grad_rows.reshape(peers, share_rows, D), 'fsdp', split_axi...]
    unnamed x6 -> x0, waiting for transfers between devices: 28.4 us -> none
  transfers between devices with their start and end apart: 10 -> 0, of which waited for: 6 -> 0; matrix products, arithmetic and copies ran while one was open for 13% -> 0% of each run, Pallas kernels for 0% -> 0%
where the time goes in v2:
time: 322 us
  Pallas kernels  304 us (94%)
  local copies, waits for them, and re-layouts  9.38 us (3%)
  other arithmetic  7.58 us (2%)
    pallas_call x1, Pallas kernels, backward_all(): pl.pallas_call(backward_kernel, out_shape=[shape((8, 64, D), low), shape(...  176 us
    pallas_call x1, Pallas kernels, forward_all(): pl.pallas_call(forward_kernel, out_shape=[shape(square, low)] * 3 + [shap...  111 us
    pallas_call x1, Pallas kernels, finish_all(): pl.pallas_call(finish_kernel, out_shape=[shape((TOK_DEV, D), low), shape(...  17.5 us
    unnamed x16, local copies, waits for them, and re-layouts  6.57 us

profile of v2, /device:TPU:9, one launch (start us, length us, event | category | flops | bytes accessed | tf_op | source)
XLA Modules:
  0.0 321.8 jit_solution(9136620202271531357)
XLA Ops:
  0.6 0.7 and_select_fusion.2
  1.3 0.2 reduce-window.4
  1.5 0.1 convert_reduce_fusion
  1.6 0.7 fusion.12
  2.2 0.7 select_reduce_fusion.1
  3.0 0.1 slice.10
  3.1 0.1 slice.9
  3.2 0.1 fusion
  3.3 0.1 reshape.302
  3.4 0.1 maximum_reduce_fusion
  3.5 0.9 add_select_fusion
  4.5 0.1 copy.59
  4.6 0.2 compare_reduce_fusion
  4.7 0.7 select_bitcast_fusion.bias
  5.4 0.8 broadcast_in_dim.97.use
  6.3 0.6 compare_convert_fusion.use_row
  6.9 1.3 fusion.3
  8.1 0.7 convert_element_type.25
  8.8 0.1 copy.58
  9.0 0.6 pad.4.vec
  9.6 0.0 copy-start.4
  9.6 110.6 %forward_all.1 = (bf16[4,2,2,48,3072]{4,3,2,1,0:T(8,128)(2,1)}, bf16[4,2,2,48,3072]{4,3,2,1,0:T(8,128)(2,1)}, bf16[4,2,2,48,3072]{4,3,2,1,0:T(8,128)(2,1)}, f32[...) custom-call(s32[1,512]{1,0:T(1,128)} %bitcast.33, ...), custom_call_target="tpu_custom_call" | custom-call | tf_op jit(solution)/shard_map/forward_all/pallas_call | solution.py:495
  120.2 0.0 copy-done.4
  120.2 0.1 select_reduce_fusion.3
  120.3 0.5 broadcast_add_fusion.block_of
  120.8 0.0 copy-start.1
  120.9 0.0 copy-start
  120.9 0.0 copy-start.2
  120.9 0.0 copy-start.3
  120.9 175.9 %backward_all.1 = (bf16[8,64,768]{2,1,0:T(8,128)(2,1)}, bf16[8,64,768]{2,1,0:T(8,128)(2,1)}, bf16[2,2,12,48,384]{4,3,2,1,0:T(8,128)(2,1)}, bf16[2,2,16,48,384]{4...) custom-call(s32[16]{0:T(128)} %broadcast_add_fusion.block_of, ...), custom_call_target="tpu_custom_call" | custom-call | tf_op jit(solution)/shard_map/backward_all/pallas_call | solution.py:1068
  296.8 0.0 copy-done.1
  296.8 0.9 copy.60.outrow
  297.7 0.0 copy-done
  297.7 0.7 copy.61.vecs
  298.4 0.0 copy-done.2
  298.4 0.7 copy.62.mom1
  299.1 0.0 copy-done.3
  299.1 0.7 copy.63.mom2
  299.8 17.5 %finish_all.1 = (bf16[512,768]{1,0:T(8,128)(2,1)}, bf16[512,768]{1,0:T(8,128)(2,1)}, f32[2,48,9216]{2,1,0:T(8,128)}, f32[2,48,9216]{2,1,0:T(8,128)}, f32[2,768,7...) custom-call(s32[12]{0:T(128)} %owner.1, ...), custom_call_target="tpu_custom_call" | custom-call | tf_op jit(solution)/shard_map/finish_all/pallas_call | solution.py:1215
  317.3 1.5 copy.64
  318.8 1.5 copy.65
  320.3 1.5 copy.66
  (6 shorter events, 0.0 us)
Async XLA Ops:
  9.6 110.6 %copy-start.4 = (s32[12]{0:T(128)S(1)}, s32[12]{0:T(128)}, u32[]{:S(2)}) copy-start(s32[12]{0:T(128)} %owner.1) | copy-start | bytes 148
  120.8 176.0 %copy-start.1 = (s32[512]{0:T(512)S(1)}, s32[512]{0:T(512)}, u32[]{:S(2)}) copy-start(s32[512]{0:T(512)} %fusion.3) | copy-start | bytes 6148
  120.9 176.8 %copy-start = (f32[96,12]{0,1:T(8,128)S(1)}, f32[96,12]{0,1:T(8,128)}, u32[]{:S(2)}) copy-start(f32[96,12]{0,1:T(8,128)} %param.21) | copy-start | bytes 13828
  120.9 177.5 %copy-start.2 = (f32[96,12]{0,1:T(8,128)S(1)}, f32[96,12]{0,1:T(8,128)}, u32[]{:S(2)}) copy-start(f32[96,12]{0,1:T(8,128)} %param.22) | copy-start | bytes 13828
  120.9 178.3 %copy-start.3 = (f32[96,12]{0,1:T(8,128)S(1)}, f32[96,12]{0,1:T(8,128)}, u32[]{:S(2)}) copy-start(f32[96,12]{0,1:T(8,128)} %param.23) | copy-start | bytes 13828
